TPU v7x, 32 devices: a whole 2x2x4 slice. The times are simulated.
32 devices in a mesh: space: 4 (over y, x), blk: 8 (over z, core).
Axes of the slice: x: 2, y: 2, z: 4, core: 2. Of those that a mesh axis runs over, the one named last changes fastest.
Arguments:
- snapshots: bfloat16 [32, 512, 3, 2048], P('blk', None, None, 'space'), may hold values from -6 to 6
- quadrature: float32 [2048], P('space'), may hold values from 0.2 to 5
- omega: float32 [16, 2, 32, 16], replicated, may hold values from -6 to 6
Outputs:
- modes: float32 [16, 2, 16, 3, 2048], P('blk', None, None, None, 'space')
- energies: float32 [16, 16], replicated
All inputs are finite; a program needn't handle non-finite values.
Results may differ from a plain program's by a relative error of at most 0.0051.
Values may be sent and summed in bfloat16 or wider, within the bound.
No kernel may reach another device: no remote copies, remote signals or barrier semaphores. Data moves between devices by JAX's collectives and lax.ppermute only.
A program may use at most 64 MiB of HBM per device.

v0:
```python
import functools
import math

import jax
import jax.numpy as jnp
import ml_dtypes
import numpy as np
from jax import lax
from jax.experimental import pallas as pl
from jax.experimental.pallas import tpu as pltpu
from jax.sharding import PartitionSpec as P

NF = 16
RANK = 16
ITERS = 2
NS_STEPS = 14
IN_FLIGHT = 6
LIMIT = 40 * 2**20
F32, BF16 = jnp.float32, jnp.bfloat16
HBM = pl.BlockSpec(memory_space=pltpu.HBM)
VMEM = pl.BlockSpec(memory_space=pltpu.VMEM)


def in_hbm(array):
    return pltpu.with_memory_space_constraint(array, pltpu.HBM)


def dft_table(sample_count, harmonic_count):
    sample = np.arange(sample_count, dtype=np.int32)
    harmonic = np.arange(1, harmonic_count + 1, dtype=np.int32)
    turns = harmonic[:, None] * sample[None, :] % sample_count
    phases = np.float32(2.0 * math.pi / sample_count) * turns.astype(np.float32)
    window = np.float32(0.5) - np.float32(0.5) * np.cos(
        np.float32(2.0 * math.pi / sample_count) * sample.astype(np.float32)
    )
    factor = np.float32(1.0) / np.sqrt(np.sum(window * window, dtype=np.float32))
    return np.stack([window * np.cos(phases) * factor, -window * np.sin(phases) * factor])


def wide_table(sample_count, groups, blocks):
    share = NF // groups
    rows = dft_table(sample_count, NF).reshape(2, groups, share, sample_count).transpose(1, 0, 2, 3)
    wide = np.zeros((groups, 2, share, blocks, blocks, sample_count), np.float32)
    for block in range(blocks):
        wide[:, :, :, block, block] = rows
    return wide.reshape(2 * NF * blocks, blocks * sample_count).astype(ml_dtypes.bfloat16)


def iota(shape, axis):
    return lax.broadcasted_iota(jnp.int32, shape, axis)


def mm(left, right, contract=(1, 0)):
    dims = (((contract[0],), (contract[1],)), ((), ()))
    return lax.dot_general(
        left, right, dims, precision=lax.Precision.HIGHEST, preferred_element_type=F32
    )


def spectra_kernel(groups, snap, table_hbm, quad_hbm, *refs):
    outs, (buf, table, quad, piles, sems, small) = refs[:-6], refs[-6:]
    blocks, comps, samples, points = snap.shape
    steps = [(c, b) for c in range(comps) for b in range(blocks)]
    copies = [
        pltpu.make_async_copy(snap.at[b, c], buf.at[b, c], sems.at[i])
        for i, (c, b) in enumerate(steps)
    ]
    table_copy = pltpu.make_async_copy(table_hbm, table, small.at[0])
    quad_copy = pltpu.make_async_copy(quad_hbm, quad, small.at[1])
    table_copy.start()
    quad_copy.start()
    for copy in copies[:IN_FLIGHT]:
        copy.start()
    me = lax.axis_index("blk")
    table_copy.wait()
    quad_copy.wait()
    root = jnp.sqrt(quad[...])
    height = piles.shape[1]
    for i, (c, b) in enumerate(steps):
        copies[i].wait()
        if i + IN_FLIGHT < len(copies):
            copies[i + IN_FLIGHT].start()
        part = jnp.dot(
            table[:, b * samples : (b + 1) * samples], buf[b, c], preferred_element_type=F32
        )
        total = part if b == 0 else total + part
        if b == blocks - 1:
            low = (total * root).astype(BF16)
            for owner in range(groups):
                piles[owner, :, c * points : (c + 1) * points] = low[
                    owner * height : (owner + 1) * height
                ]
    for far, out in enumerate(outs):
        for core in range(2):
            out[core] = piles[me ^ (2 * far + core)]


def start_kernel(share, blocks, omega, _, out, own, sem):
    me = lax.axis_index("blk")
    copy = pltpu.make_async_copy(omega.at[pl.ds(me * share, share)], own, sem)
    copy.start()
    copy.wait()
    total = own.shape[-1]
    half = share * blocks
    rows = 2 * share * total
    row, col = iota((rows, total), 0), iota((rows, total), 1)
    source, part, freq, block = row // (2 * half), row // half % 2, row // blocks % share, row % blocks
    hit = (source ^ me) * blocks + block == col
    columns = []
    for f in range(share):
        real, imag = own[f, 0], own[f, 1]
        for first, second in ((real, imag), (-imag, real)):
            upper = jnp.where(hit & (freq == f) & (part == 0), 1.0, 0.0)
            lower = jnp.where(hit & (freq == f) & (part == 1), 1.0, 0.0)
            columns.append(mm(upper, first, (1, 1)) + mm(lower, second, (1, 1)))
    for i, column in enumerate(columns):
        out[:, i * RANK : (i + 1) * RANK] = column


def swap_lanes(value, half):
    width = value.shape[-1]
    axis = value.ndim - 1
    lane = iota(value.shape, axis)
    down = pltpu.roll(value, half, axis)
    up = pltpu.roll(value, width - half, axis)
    return jnp.where(lane // half % 2 == 0, up, down)


def stacked(refs):
    if refs[0].shape[0] % 16 == 0:
        return jnp.concatenate([ref[...] for ref in refs], 0)
    return jnp.concatenate([ref[...].astype(F32) for ref in refs], 0).astype(BF16)


def gram_kernel(share, blocks, *refs):
    pieces, out = refs[:-1], refs[-1]
    half = share * blocks
    data = stacked(pieces)
    size = data.shape[0]
    products = lax.dot_general(data, data, (((1,), (1,)), ((), ())), preferred_element_type=F32)
    if half != 8:
        row, lane = iota((size, size), 0), iota((size, size), 1)
        turned = swap_lanes(products, half)
        down, up = pltpu.roll(turned, half, 0), pltpu.roll(turned, size - half, 0)
        same = (row // half + lane // half) % 2 == 0
        out[...] = jnp.where(same, products, -products) + jnp.where(row // half % 2 == 0, up, down)
        return
    sources = size // 16
    products = products.reshape(sources, 2, 8, size)
    shape = (sources, 8, size)
    row, lane = iota(shape, 1), iota(shape, 2)
    real = products[:, 0]
    value = jnp.where(lane // half % 2 == 0, real, -real) + swap_lanes(products[:, 1], half)
    value = jnp.where(row // blocks == lane // blocks % share, value, 0.0)
    if share == 2:
        value = (value + pltpu.roll(value, 4, 1)).reshape(sources // 2, 2, 8, size)
        value = jnp.where(iota((sources // 2, 8, size), 1) < 4, value[:, 0], value[:, 1])
    out[...] = value.reshape(out.shape)


def spread_gram(value, share, blocks):
    half = share * blocks
    size = value.shape[-1]
    if half != 8:
        row, lane = iota((size, size), 0), iota((size, size), 1)
        return jnp.where(row // blocks % share == lane // blocks % share, value, 0.0)
    sources = size // 16
    shape = (sources, 8, size)
    row, lane = iota(shape, 1), iota(shape, 2)
    if share == 2:
        value = value.reshape(sources // 2, 8, size)
        other = pltpu.roll(value, 4, 1)
        low = iota(value.shape, 1) < 4
        value = jnp.stack([jnp.where(low, value, other), jnp.where(low, other, value)], 1)
    value = value.reshape(shape)
    value = jnp.where(row // blocks == lane // blocks % share, value, 0.0)
    turned = swap_lanes(value, half)
    turned = jnp.where(lane // half % 2 == 0, -turned, turned)
    return jnp.stack([value, turned], 1).reshape(size, size)


def inverse_root(inner, share):
    size = inner.shape[0]
    width = size // share
    identity = jnp.where(iota((size, size), 0) == iota((size, size), 1), 1.0, 0.0)
    norms = []
    for f in range(share):
        block = inner[f * width : (f + 1) * width]
        norms.append(jnp.broadcast_to(jnp.sqrt(jnp.sum(block * block, keepdims=True)), block.shape))
    norm = norms[0] if share == 1 else jnp.concatenate(norms, 0)
    joint = inner / norm
    inverse = None
    for step in range(NS_STEPS):
        factor = 1.5 * identity - 0.5 * joint
        if step < NS_STEPS - 1:
            joint = mm(mm(joint, factor), factor)
        inverse = factor if step == 0 else mm(factor, inverse)
    return inverse / jnp.sqrt(norm)


def subspace_kernel(share, blocks, dofs, grams, *refs):
    parts, (start, coef_out, energy_out) = refs[:grams], refs[grams:]
    value = parts[0][...]
    for part in parts[1:]:
        value = value + part[...]
    gram = spread_gram(value * (1.0 / dofs), share, blocks)
    nxt = mm(gram, start[...])
    for step in range(ITERS):
        image = mm(gram, nxt)
        root = inverse_root(mm(nxt, image, (0, 0)), share)
        if step < ITERS - 1:
            nxt = mm(image, root)
    coef, image = mm(nxt, root), mm(image, root)
    half = share * blocks
    row, lane = iota(coef.shape, 0), iota(coef.shape, 1)
    same = (row // half + lane // RANK) % 2 == 0
    coef_out[...] = jnp.where(same, coef, -coef).astype(BF16)
    energy = jnp.sum(image * image, axis=0, keepdims=True)
    me = lax.axis_index("blk")
    energy_out[...] = jnp.zeros_like(energy_out)
    for f in range(share):
        energy_out[pl.ds(me * share + f, 1), :] = energy[:, 2 * f * RANK : (2 * f + 1) * RANK]


def modes_kernel(share, quad, coef, *refs):
    pieces, out = refs[:-1], refs[-1]
    data = stacked(pieces)
    points = quad.shape[-1]
    inverse = 1.0 / jnp.sqrt(quad[...])
    for c in range(data.shape[-1] // points):
        modes = lax.dot_general(
            coef[...],
            data[:, c * points : (c + 1) * points],
            (((0,), (0,)), ((), ())),
            preferred_element_type=F32,
        )
        modes = modes * inverse
        for f in range(share):
            for part in range(2):
                at = (2 * f + part) * RANK
                out[f, part, c] = modes[at : at + RANK]


def call(kernel, outs, specs, name, scratch=()):
    return pl.pallas_call(
        kernel,
        out_shape=outs,
        in_specs=specs,
        out_specs=jax.tree.map(lambda _: VMEM, outs),
        scratch_shapes=list(scratch),
        compiler_params=pltpu.CompilerParams(vmem_limit_bytes=LIMIT),
        name=name,
    )


def exchange(array, axis, distance):
    size = lax.axis_size(axis)
    return lax.ppermute(array, axis, [(i, i ^ distance) for i in range(size)])


def per_device(snapshots, quadrature, omega):
    blocks, samples, comps, points = snapshots.shape
    groups, spaces = lax.axis_size("blk"), lax.axis_size("space")
    share = NF // groups
    reach = groups // 2
    height = 2 * share * blocks
    width = comps * points
    size = groups * height
    piece = (height, width)

    table = in_hbm(jnp.asarray(wide_table(samples, groups, blocks)))
    quad = quadrature.reshape(1, points)
    steps = blocks * comps
    spectra = call(
        functools.partial(spectra_kernel, groups),
        [jax.ShapeDtypeStruct((2, *piece), BF16)] * reach,
        [HBM] * 3,
        "spectra",
        [
            pltpu.VMEM((blocks, comps, samples, points), BF16),
            pltpu.VMEM(table.shape, BF16),
            pltpu.VMEM((1, points), F32),
            pltpu.VMEM((groups, *piece), BF16),
            pltpu.SemaphoreType.DMA((steps,)),
            pltpu.SemaphoreType.DMA((2,)),
        ],
    )(in_hbm(snapshots.transpose(0, 2, 1, 3)), table, in_hbm(quad))

    start = call(
        functools.partial(start_kernel, share, blocks),
        jax.ShapeDtypeStruct((size, 2 * share * RANK), F32),
        [HBM, pl.BlockSpec(memory_space=pl.ANY)],
        "start",
        [pltpu.VMEM((share, 2, RANK, groups * blocks), F32), pltpu.SemaphoreType.DMA],
    )(in_hbm(omega.transpose(0, 1, 3, 2)), spectra[0])

    pieces = [None] * groups
    pieces[0] = spectra[0][0]
    arrived = {far: exchange(spectra[far], "blk", 2 * far) for far in range(reach - 1, 0, -1)}
    pieces[1] = exchange(spectra[0][1], "blk", 1)
    for far in range(reach - 1, 0, -1):
        pieces[2 * far] = arrived[far][0]
        pieces[2 * far + 1] = exchange(arrived[far][1], "blk", 1)

    packed = (size * (blocks if share * blocks == 8 else height) // height, size)
    gram = call(
        functools.partial(gram_kernel, share, blocks),
        jax.ShapeDtypeStruct(packed, F32),
        [VMEM] * groups,
        "gram",
    )(*pieces)
    if spaces <= 4:
        grams = [gram] + [exchange(gram, "space", d) for d in range(spaces - 1, 0, -1)]
    else:
        grams = [lax.psum(gram, "space")]

    coef, energies = call(
        functools.partial(subspace_kernel, share, blocks, width * spaces, len(grams)),
        [
            jax.ShapeDtypeStruct((size, 2 * share * RANK), BF16),
            jax.ShapeDtypeStruct((NF, RANK), F32),
        ],
        [VMEM] * (len(grams) + 1),
        "subspace",
    )(*grams, start)

    modes = call(
        functools.partial(modes_kernel, share),
        jax.ShapeDtypeStruct((share, 2, comps, RANK, points), F32),
        [VMEM] * (groups + 2),
        "modes",
    )(quad, coef, *pieces)

    energies = energies + exchange(energies, "blk", 1)
    shares = [exchange(energies, "blk", 2 * far) for far in range(reach - 1, 0, -1)]
    for other in shares:
        energies = energies + other
    return modes.transpose(0, 1, 3, 2, 4), energies


def solution(mesh):
    in_specs = (P("blk", None, None, "space"), P("space"), P())
    out_specs = (P("blk", None, None, None, "space"), P())
    return jax.shard_map(
        per_device, mesh=mesh, in_specs=in_specs, out_specs=out_specs, check_vma=False
    )
```

profile of v0, /device:TPU:0, one launch (start us, length us, event | category | flops | bytes accessed | tf_op | source)
XLA Modules:
  0.0 49.5 jit_solution(8368024021142405879)
XLA Ops:
  0.6 0.0 copy-start
  0.6 4.1 %spectra.1 = (bf16[2,16,1536]{2,1,0:T(8,128)(2,1)S(1)}, bf16[2,16,1536]{2,1,0:T(8,128)(2,1)S(1)}, bf16[2,16,1536]{2,1,0:T(8,128)(2,1)S(1)}, bf16[2,16,1536]{2,1,0:T(8,128)(2,1)S(1)}) custom-call(bf16[4,3,512,512]{3,2,1,0:T(8,128)(2,1)} %bitcast.22, bf16[128,2048]{1,0:T(8,128)(2,1)} %constant.2.clone.table_hbm, f32[1,512]{1,0:T(1,128)} %bitcast.20), custom_call_target="tpu_custom_call" | custom-call | tf_op jit(solution)/shard_map/spectra/pallas_call | solution.py:274
  4.7 3.1 %collective-permute-start.1 = (bf16[2,16,1536]{2,1,0:T(8,128)(2,1)S(1)}, bf16[2,16,1536]{2,1,0:T(8,128)(2,1)S(1)}, u32[]{:S(2)}, u32[]{:S(2)}) collective-permute-start(bf16[2,16,1536]{2,1,0:T(8,128)(2,1)S(1)} %get-tuple-element.9), channel_id=1, source_target_pairs={{0,2},{1,3},{2,0},{3,1},{4,6},{5,7},{6,4},{7,5},{8,10},{9,11},{10,... | collective-permute-start | bytes 294920 | tf_op jit(solution)/shard_map/ppermute | solution.py:258
  7.8 0.1 collective-permute-start
  7.9 2.7 %collective-permute-start.3 = (bf16[2,16,1536]{2,1,0:T(8,128)(2,1)S(1)}, bf16[2,16,1536]{2,1,0:T(8,128)(2,1)S(1)}, u32[]{:S(2)}, u32[]{:S(2)}) collective-permute-start(bf16[2,16,1536]{2,1,0:T(8,128)(2,1)S(1)} %get-tuple-element.10), channel_id=1, source_target_pairs={{0,4},{1,5},{2,6},{3,7},{4,0},{5,1},{6,2},{7,3},{8,12},{9,13},{10,... | collective-permute-start | bytes 294920 | tf_op jit(solution)/shard_map/ppermute | solution.py:258
  10.5 0.0 collective-permute-start.5
  10.5 0.1 collective-permute-done.1
  10.6 0.2 collective-permute-start.2
  10.8 7.5 %collective-permute-done.3 = bf16[2,16,1536]{2,1,0:T(8,128)(2,1)S(1)} collective-permute-done((bf16[2,16,1536]{2,1,0:T(8,128)(2,1)S(1)}, bf16[2,16,1536]{2,1,0:T(8,128)(2,1)S(1)}, u32[]{:S(2)}, u32[]{:S(2)}) %collective-permute-start.3) | collective-permute-done | bytes 98336 | tf_op jit(solution)/shard_map/ppermute | solution.py:258
  18.4 0.1 collective-permute-start.4
  18.4 0.0 collective-permute-done.5
  18.5 0.5 %collective-permute-start.6 = (bf16[16,1536]{1,0:T(8,128)(2,1)S(1)}, bf16[16,1536]{1,0:T(8,128)(2,1)S(1)}, u32[]{:S(2)}, u32[]{:S(2)}) collective-permute-start(bf16[16,1536]{1,0:T(8,128)(2,1)S(1)} %get-tuple-element.14), channel_id=1, source_target_pairs={{0,1},{1,0},{2,3},{3,2},{4,5},{5,4},{6,7},{7,6},{8,9},{9,8},{10,11... | collective-permute-start | bytes 147464 | tf_op jit(solution)/shard_map/ppermute | solution.py:258
  19.0 0.0 collective-permute-done.refs_1_
  19.0 0.0 collective-permute-done.2.refs_3_
  19.0 0.6 %collective-permute-done.4.refs_5_ = bf16[16,1536]{1,0:T(8,128)(2,1)S(1)} collective-permute-done((bf16[16,1536]{1,0:T(8,128)(2,1)S(1)}, bf16[16,1536]{1,0:T(8,128)(2,1)S(1)}, u32[]{:S(2)}, u32[]{:S(2)}) %collective-permute-start.4) | collective-permute-done | bytes 49184 | tf_op jit(solution)/shard_map/ppermute | solution.py:258
  19.7 0.2 collective-permute-done.6.refs_7_
  19.9 0.3 gram.1.refs_0_
  20.2 1.6 %collective-permute-start.9 = (f32[32,128]{1,0:T(8,128)S(1)}, f32[32,128]{1,0:T(8,128)S(1)}, u32[]{:S(2)}, u32[]{:S(2)}) collective-permute-start(f32[32,128]{1,0:T(8,128)S(1)} %gram.1.refs_0_), channel_id=1, source_target_pairs={{0,8},{8,0},{16,24},{24,16},{1,9},{9,1},{17,25},{25,17},{2,10},{10... | collective-permute-start | bytes 49160 | tf_op jit(solution)/shard_map/ppermute | solution.py:258
  21.8 1.5 %collective-permute-start.8 = (f32[32,128]{1,0:T(8,128)S(1)}, f32[32,128]{1,0:T(8,128)S(1)}, u32[]{:S(2)}, u32[]{:S(2)}) collective-permute-start(f32[32,128]{1,0:T(8,128)S(1)} %gram.1.refs_0_), channel_id=1, source_target_pairs={{0,16},{8,24},{16,0},{24,8},{1,17},{9,25},{17,1},{25,9},{2,18},{10... | collective-permute-start | bytes 49160 | tf_op jit(solution)/shard_map/ppermute | solution.py:258
  23.4 0.4 collective-permute-start.7
  23.8 1.4 %start.1.refs_4_ = f32[128,64]{1,0:T(8,128)S(1)} custom-call(f32[16,2,16,32]{3,2,1,0:T(8,128)} %bitcast.24, bf16[2,16,1536]{2,1,0:T(8,128)(2,1)S(1)} %get-tuple-element.8._), custom_call_target="tpu_custom_call" | custom-call | tf_op jit(solution)/shard_map/start/pallas_call | solution.py:289
  25.2 0.0 collective-permute-done.9.refs_3_
  25.2 0.3 collective-permute-done.8.refs_2_
  25.6 2.4 %collective-permute-done.7.refs_1_ = f32[32,128]{1,0:T(8,128)S(1)} collective-permute-done((f32[32,128]{1,0:T(8,128)S(1)}, f32[32,128]{1,0:T(8,128)S(1)}, u32[]{:S(2)}, u32[]{:S(2)}) %collective-permute-start.7) | collective-permute-done | bytes 16416 | tf_op jit(solution)/shard_map/ppermute | solution.py:258
  28.0 10.9 %subspace.1 = (bf16[128,64]{1,0:T(8,128)(2,1)S(1)}, f32[16,16]{1,0:T(8,128)S(1)}) custom-call(f32[32,128]{1,0:T(8,128)S(1)} %gram.1.refs_0_, f32[32,128]{1,0:T(8,128)S(1)} %collective-permute-done.7.refs_1_, f32[32,128]{1,0:T(8,128)S(1)} %collective-permute-done.8.refs_2_, f32[32,128]{1,0:T(8,128)S(1)} %collective-permute-done.9.refs_3_, ...), custom_call_target="tpu_custom_call" | custom-call | tf_op jit(solution)/shard_map/subspace/pallas_call | solution.py:317
  38.9 0.0 collective-permute-start.10
  39.0 1.2 %collective-permute-done.10 = f32[16,16]{1,0:T(8,128)S(1)} collective-permute-done((f32[16,16]{1,0:T(8,128)S(1)}, f32[16,16]{1,0:T(8,128)S(1)}, u32[]{:S(2)}, u32[]{:S(2)}) %collective-permute-start.10) | collective-permute-done | bytes 1056 | tf_op jit(solution)/shard_map/ppermute | solution.py:258
  40.1 2.2 %collective-permute-start.13 = (f32[16,16]{1,0:T(8,128)S(1)}, f32[16,16]{1,0:T(8,128)S(1)}, u32[]{:S(2)}, u32[]{:S(2)}) collective-permute-start(f32[16,16]{1,0:T(8,128)S(1)} %add.12), channel_id=1, source_target_pairs={{0,2},{1,3},{2,0},{3,1},{4,6},{5,7},{6,4},{7,5},{8,10},{9,11},{10,... | collective-permute-start | bytes 3080 | tf_op jit(solution)/shard_map/ppermute | solution.py:258
  42.3 1.2 %collective-permute-start.12 = (f32[16,16]{1,0:T(8,128)S(1)}, f32[16,16]{1,0:T(8,128)S(1)}, u32[]{:S(2)}, u32[]{:S(2)}) collective-permute-start(f32[16,16]{1,0:T(8,128)S(1)} %add.12), channel_id=1, source_target_pairs={{0,4},{1,5},{2,6},{3,7},{4,0},{5,1},{6,2},{7,3},{8,12},{9,13},{10,... | collective-permute-start | bytes 3080 | tf_op jit(solution)/shard_map/ppermute | solution.py:258
  43.5 1.4 %collective-permute-start.11 = (f32[16,16]{1,0:T(8,128)S(1)}, f32[16,16]{1,0:T(8,128)S(1)}, u32[]{:S(2)}, u32[]{:S(2)}) collective-permute-start(f32[16,16]{1,0:T(8,128)S(1)} %add.12), channel_id=1, source_target_pairs={{0,6},{1,7},{2,4},{3,5},{4,2},{5,3},{6,0},{7,1},{8,14},{9,15},{10,... | collective-permute-start | bytes 3080 | tf_op jit(solution)/shard_map/ppermute | solution.py:258
  44.9 0.0 copy-done
  44.9 1.0 %modes.1 = f32[2,2,3,16,512]{4,3,2,1,0:T(8,128)} custom-call(f32[1,512]{1,0:T(1,128)S(1)} %bitcast.21, bf16[128,64]{1,0:T(8,128)(2,1)S(1)} %get-tuple-element.12.coef, bf16[16,1536]{1,0:T(8,128)(2,1)S(1)} %get-tuple-element.21.refs_0_, bf16[16,1536]{1,0:T(8,128)(2,1)S(1)} %collective-permute-done.refs_1_, bf16[16,1536]{1,0:T(8,128)(2,1)S(1)} %get-tuple-element.19.refs_2_, ...), custom_call_target="tpu_custom_call" | custom-call | tf_op jit(solution)/shard_map/modes/pallas_call | solution.py:327
  45.9 0.0 collective-permute-done.13
  45.9 1.0 %collective-permute-done.12 = f32[16,16]{1,0:T(8,128)S(1)} collective-permute-done((f32[16,16]{1,0:T(8,128)S(1)}, f32[16,16]{1,0:T(8,128)S(1)}, u32[]{:S(2)}, u32[]{:S(2)}) %collective-permute-start.12) | collective-permute-done | bytes 1056 | tf_op jit(solution)/shard_map/ppermute | solution.py:258
  46.9 2.1 %collective-permute-done.11 = f32[16,16]{1,0:T(8,128)S(1)} collective-permute-done((f32[16,16]{1,0:T(8,128)S(1)}, f32[16,16]{1,0:T(8,128)S(1)}, u32[]{:S(2)}, u32[]{:S(2)}) %collective-permute-start.11) | collective-permute-done | bytes 1056 | tf_op jit(solution)/shard_map/ppermute | solution.py:258
  48.9 0.6 %add_add_fusion = f32[16,16]{1,0:T(8,128)} fusion(f32[16,16]{1,0:T(8,128)S(1)} %collective-permute-done.13, f32[16,16]{1,0:T(8,128)S(1)} %collective-permute-done.12, f32[16,16]{1,0:T(8,128)S(1)} %add.12, f32[16,16]{1,0:T(8,128)S(1)} %collective-permute-done.11), kind=kLoop, calls=%fused_computation.8 | loop fusion | flops 768 | bytes 5120 | tf_op jit(solution)/shard_map/add | solution.py:337
  (5 shorter events, 0.0 us)
Async XLA Ops:
  0.6 44.3 %copy-start = (f32[512]{0:T(512)S(1)}, f32[512]{0:T(512)}, u32[]{:S(2)}) copy-start(f32[512]{0:T(512)} %param.5) | copy-start | bytes 6148
  4.7 5.9 %collective-permute-start.1 = (bf16[2,16,1536]{2,1,0:T(8,128)(2,1)S(1)}, bf16[2,16,1536]{2,1,0:T(8,128)(2,1)S(1)}, u32[]{:S(2)}, u32[]{:S(2)}) collective-permute-start(bf16[2,16,1536]{2,1,0:T(8,128)(2,1)S(1)} %get-tuple-element.9), channel_id=1, source_target_pairs={{0,2},{1,3},{2,0},{3,1},{4,6},{5,7},{6,4},{7,5},{8,10},{9,11},{10,... | collective-permute-start | bytes 294920 | tf_op jit(solution)/shard_map/ppermute | solution.py:258
  7.8 11.2 %collective-permute-start = (bf16[16,1536]{1,0:T(8,128)(2,1)S(1)}, bf16[16,1536]{1,0:T(8,128)(2,1)S(1)}, u32[]{:S(2)}, u32[]{:S(2)}) collective-permute-start(bf16[16,1536]{1,0:T(8,128)(2,1)S(1)} %get-tuple-element.20), channel_id=1, source_target_pairs={{0,1},{1,0},{2,3},{3,2},{4,5},{5,4},{6,7},{7,6},{8,9},{9,8},{10,11... | collective-permute-start | bytes 147464 | tf_op jit(solution)/shard_map/ppermute | solution.py:258
  7.9 10.5 %collective-permute-start.3 = (bf16[2,16,1536]{2,1,0:T(8,128)(2,1)S(1)}, bf16[2,16,1536]{2,1,0:T(8,128)(2,1)S(1)}, u32[]{:S(2)}, u32[]{:S(2)}) collective-permute-start(bf16[2,16,1536]{2,1,0:T(8,128)(2,1)S(1)} %get-tuple-element.10), channel_id=1, source_target_pairs={{0,4},{1,5},{2,6},{3,7},{4,0},{5,1},{6,2},{7,3},{8,12},{9,13},{10,... | collective-permute-start | bytes 294920 | tf_op jit(solution)/shard_map/ppermute | solution.py:258
  10.5 7.9 %collective-permute-start.5 = (bf16[2,16,1536]{2,1,0:T(8,128)(2,1)S(1)}, bf16[2,16,1536]{2,1,0:T(8,128)(2,1)S(1)}, u32[]{:S(2)}, u32[]{:S(2)}) collective-permute-start(bf16[2,16,1536]{2,1,0:T(8,128)(2,1)S(1)} %get-tuple-element.11), channel_id=1, source_target_pairs={{0,6},{1,7},{2,4},{3,5},{4,2},{5,3},{6,0},{7,1},{8,14},{9,15},{10,... | collective-permute-start | bytes 294920 | tf_op jit(solution)/shard_map/ppermute | solution.py:258
  10.6 8.4 %collective-permute-start.2 = (bf16[16,1536]{1,0:T(8,128)(2,1)S(1)}, bf16[16,1536]{1,0:T(8,128)(2,1)S(1)}, u32[]{:S(2)}, u32[]{:S(2)}) collective-permute-start(bf16[16,1536]{1,0:T(8,128)(2,1)S(1)} %get-tuple-element.18), channel_id=1, source_target_pairs={{0,1},{1,0},{2,3},{3,2},{4,5},{5,4},{6,7},{7,6},{8,9},{9,8},{10,11... | collective-permute-start | bytes 147464 | tf_op jit(solution)/shard_map/ppermute | solution.py:258
  18.4 1.3 %collective-permute-start.4 = (bf16[16,1536]{1,0:T(8,128)(2,1)S(1)}, bf16[16,1536]{1,0:T(8,128)(2,1)S(1)}, u32[]{:S(2)}, u32[]{:S(2)}) collective-permute-start(bf16[16,1536]{1,0:T(8,128)(2,1)S(1)} %get-tuple-element.16), channel_id=1, source_target_pairs={{0,1},{1,0},{2,3},{3,2},{4,5},{5,4},{6,7},{7,6},{8,9},{9,8},{10,11... | collective-permute-start | bytes 147464 | tf_op jit(solution)/shard_map/ppermute | solution.py:258
  18.5 1.4 %collective-permute-start.6 = (bf16[16,1536]{1,0:T(8,128)(2,1)S(1)}, bf16[16,1536]{1,0:T(8,128)(2,1)S(1)}, u32[]{:S(2)}, u32[]{:S(2)}) collective-permute-start(bf16[16,1536]{1,0:T(8,128)(2,1)S(1)} %get-tuple-element.14), channel_id=1, source_target_pairs={{0,1},{1,0},{2,3},{3,2},{4,5},{5,4},{6,7},{7,6},{8,9},{9,8},{10,11... | collective-permute-start | bytes 147464 | tf_op jit(solution)/shard_map/ppermute | solution.py:258
  20.2 5.0 %collective-permute-start.9 = (f32[32,128]{1,0:T(8,128)S(1)}, f32[32,128]{1,0:T(8,128)S(1)}, u32[]{:S(2)}, u32[]{:S(2)}) collective-permute-start(f32[32,128]{1,0:T(8,128)S(1)} %gram.1.refs_0_), channel_id=1, source_target_pairs={{0,8},{8,0},{16,24},{24,16},{1,9},{9,1},{17,25},{25,17},{2,10},{10... | collective-permute-start | bytes 49160 | tf_op jit(solution)/shard_map/ppermute | solution.py:258
  21.8 3.7 %collective-permute-start.8 = (f32[32,128]{1,0:T(8,128)S(1)}, f32[32,128]{1,0:T(8,128)S(1)}, u32[]{:S(2)}, u32[]{:S(2)}) collective-permute-start(f32[32,128]{1,0:T(8,128)S(1)} %gram.1.refs_0_), channel_id=1, source_target_pairs={{0,16},{8,24},{16,0},{24,8},{1,17},{9,25},{17,1},{25,9},{2,18},{10... | collective-permute-start | bytes 49160 | tf_op jit(solution)/shard_map/ppermute | solution.py:258
  23.4 4.6 %collective-permute-start.7 = (f32[32,128]{1,0:T(8,128)S(1)}, f32[32,128]{1,0:T(8,128)S(1)}, u32[]{:S(2)}, u32[]{:S(2)}) collective-permute-start(f32[32,128]{1,0:T(8,128)S(1)} %gram.1.refs_0_), channel_id=1, source_target_pairs={{0,24},{8,16},{16,8},{24,0},{1,25},{9,17},{17,9},{25,1},{2,26},{10... | collective-permute-start | bytes 49160 | tf_op jit(solution)/shard_map/ppermute | solution.py:258
  38.9 1.2 %collective-permute-start.10 = (f32[16,16]{1,0:T(8,128)S(1)}, f32[16,16]{1,0:T(8,128)S(1)}, u32[]{:S(2)}, u32[]{:S(2)}) collective-permute-start(f32[16,16]{1,0:T(8,128)S(1)} %get-tuple-element.13), channel_id=1, source_target_pairs={{0,1},{1,0},{2,3},{3,2},{4,5},{5,4},{6,7},{7,6},{8,9},{9,8},{10,11... | collective-permute-start | bytes 3080 | tf_op jit(solution)/shard_map/ppermute | solution.py:258
  40.1 5.7 %collective-permute-start.13 = (f32[16,16]{1,0:T(8,128)S(1)}, f32[16,16]{1,0:T(8,128)S(1)}, u32[]{:S(2)}, u32[]{:S(2)}) collective-permute-start(f32[16,16]{1,0:T(8,128)S(1)} %add.12), channel_id=1, source_target_pairs={{0,2},{1,3},{2,0},{3,1},{4,6},{5,7},{6,4},{7,5},{8,10},{9,11},{10,... | collective-permute-start | bytes 3080 | tf_op jit(solution)/shard_map/ppermute | solution.py:258
  42.3 4.5 %collective-permute-start.12 = (f32[16,16]{1,0:T(8,128)S(1)}, f32[16,16]{1,0:T(8,128)S(1)}, u32[]{:S(2)}, u32[]{:S(2)}) collective-permute-start(f32[16,16]{1,0:T(8,128)S(1)} %add.12), channel_id=1, source_target_pairs={{0,4},{1,5},{2,6},{3,7},{4,0},{5,1},{6,2},{7,3},{8,12},{9,13},{10,... | collective-permute-start | bytes 3080 | tf_op jit(solution)/shard_map/ppermute | solution.py:258
  43.5 5.4 %collective-permute-start.11 = (f32[16,16]{1,0:T(8,128)S(1)}, f32[16,16]{1,0:T(8,128)S(1)}, u32[]{:S(2)}, u32[]{:S(2)}) collective-permute-start(f32[16,16]{1,0:T(8,128)S(1)} %add.12), channel_id=1, source_target_pairs={{0,6},{1,7},{2,4},{3,5},{4,2},{5,3},{6,0},{7,1},{8,14},{9,15},{10,... | collective-permute-start | bytes 3080 | tf_op jit(solution)/shard_map/ppermute | solution.py:258
where the time goes:
time: 49.7 us; the launch traced here: 49.5 us
  Pallas kernels  17.8 us (36%)
  waiting for transfers between devices  15.5 us (31%)
  starting transfers between devices  14.9 us (30%)
  between operations  0.73 us (1%)
  other arithmetic  0.61 us (1%)
    ppermute x14, waiting for transfers between devices, exchange(): return lax.ppermute(array, axis, [(i, i ^ distance) for i in range(size)])  15.5 us
    ppermute x14, starting transfers between devices, exchange(): return lax.ppermute(array, axis, [(i, i ^ distance) for i in range(size)])  14.9 us
    pallas_call x1, Pallas kernels, per_device(): call(functools.partial(subspace_kernel, share, blocks, width * spaces, le...  10.9 us
    pallas_call x1, Pallas kernels, per_device(): call(functools.partial(spectra_kernel, groups), [jax.ShapeDtypeStruct((2,...  4.07 us
    pallas_call x1, Pallas kernels, per_device(): call(functools.partial(start_kernel, share, blocks), jax.ShapeDtypeStruct...  1.42 us
  transfers between devices with their start and end apart: 14, of which 9 were waited for; matrix products, arithmetic and copies ran while one was open for 0% of the time, Pallas kernels for 5%

commit v1 on v0

--- a/solution.py
+++ b/solution.py
@@ -14,6 +14,9 @@
 RANK = 16
 ITERS = 2
 NS_STEPS = 14
+FULL_STEPS = 6
+WIDTH = 2 * RANK
+COPIES = 4
 IN_FLIGHT = 6
 LIMIT = 40 * 2**20
 F32, BF16 = jnp.float32, jnp.bfloat16
@@ -95,26 +98,30 @@
             out[core] = piles[me ^ (2 * far + core)]
 
 
-def start_kernel(share, blocks, omega, _, out, own, sem):
+def start_kernel(share, blocks, omega, _, wide_out, tall_out, own, sem):
     me = lax.axis_index("blk")
     copy = pltpu.make_async_copy(omega.at[pl.ds(me * share, share)], own, sem)
     copy.start()
     copy.wait()
     total = own.shape[-1]
     half = share * blocks
-    rows = 2 * share * total
-    row, col = iota((rows, total), 0), iota((rows, total), 1)
-    source, part, freq, block = row // (2 * half), row // half % 2, row // blocks % share, row % blocks
-    hit = (source ^ me) * blocks + block == col
-    columns = []
+    size = 2 * share * total
+
+    def placed(shape, axis, f, part):
+        index, block = iota(shape, axis), iota(shape, 1 - axis)
+        same = ((index // (2 * half)) ^ me) * blocks + index % blocks == block
+        return jnp.where(same & (index // blocks % share == f) & (index // half % 2 == part), 1.0, 0.0)
+
     for f in range(share):
         real, imag = own[f, 0], own[f, 1]
-        for first, second in ((real, imag), (-imag, real)):
-            upper = jnp.where(hit & (freq == f) & (part == 0), 1.0, 0.0)
-            lower = jnp.where(hit & (freq == f) & (part == 1), 1.0, 0.0)
-            columns.append(mm(upper, first, (1, 1)) + mm(lower, second, (1, 1)))
-    for i, column in enumerate(columns):
-        out[:, i * RANK : (i + 1) * RANK] = column
+        first = jnp.concatenate([real, -imag], 0)
+        second = jnp.concatenate([imag, real], 0)
+        wide_out[f] = mm(
+            placed((size, total), 0, f, 0), jnp.concatenate([first] * COPIES, 0), (1, 1)
+        ) + mm(placed((size, total), 0, f, 1), jnp.concatenate([second] * COPIES, 0), (1, 1))
+        tall_out[f * WIDTH : (f + 1) * WIDTH] = mm(
+            first, placed((total, size), 1, f, 0)
+        ) + mm(second, placed((total, size), 1, f, 1))
 
 
 def swap_lanes(value, half):
@@ -179,47 +186,83 @@
     return jnp.stack([value, turned], 1).reshape(size, size)
 
 
-def inverse_root(inner, share):
-    size = inner.shape[0]
-    width = size // share
-    identity = jnp.where(iota((size, size), 0) == iota((size, size), 1), 1.0, 0.0)
-    norms = []
-    for f in range(share):
-        block = inner[f * width : (f + 1) * width]
-        norms.append(jnp.broadcast_to(jnp.sqrt(jnp.sum(block * block, keepdims=True)), block.shape))
-    norm = norms[0] if share == 1 else jnp.concatenate(norms, 0)
-    joint = inner / norm
-    inverse = None
-    for step in range(NS_STEPS):
-        factor = 1.5 * identity - 0.5 * joint
-        if step < NS_STEPS - 1:
-            joint = mm(mm(joint, factor), factor)
-        inverse = factor if step == 0 else mm(factor, inverse)
-    return inverse / jnp.sqrt(norm)
+def thirds(value):
+    high = value.astype(BF16)
+    rest = value - high.astype(F32)
+    middle = rest.astype(BF16)
+    return high, middle, (rest - middle.astype(F32)).astype(BF16)
+
+
+def packed_mm(left, right, full=True):
+    high, middle, low = thirds(left)
+    group = iota(left.shape, 1) // WIDTH
+    first = jnp.where(group == 2, middle, high)
+    top, mid, end = right
+    total = jnp.dot(first, jnp.concatenate([top, mid, top, end], 0), preferred_element_type=F32)
+    if full:
+        second = jnp.where(group == 0, middle, low)[:, : 2 * WIDTH]
+        total = total + jnp.dot(second, jnp.concatenate([mid, top], 0), preferred_element_type=F32)
+    return total
+
+
+def inverse_roots(inners):
+    shape = inners[0].shape
+    identity = jnp.where(iota(shape, 0) == iota(shape, 1) % WIDTH, 1.0, 0.0)
+    norms = [
+        jnp.sqrt(jnp.sum(inner * inner, keepdims=True) * (1.0 / COPIES)) for inner in inners
+    ]
+    rests = [identity - inner / norm for inner, norm in zip(inners, norms)]
+    roots = [identity + 0.5 * rest for rest in rests]
+    for step in range(1, NS_STEPS):
+        full = step <= FULL_STEPS
+        rights = [thirds(rest) for rest in rests]
+        squares = [packed_mm(e, r, full) for e, r in zip(rests, rights)]
+        cubes = [packed_mm(s, r, full) for s, r in zip(squares, rights)]
+        if step > 1:
+            roots = [z + 0.5 * packed_mm(z, r, full) for z, r in zip(roots, rights)]
+        rests = [0.75 * s + 0.25 * c for s, c in zip(squares, cubes)]
+    rights = [thirds(rest) for rest in rests]
+    roots = [z + 0.5 * packed_mm(z, r, False) for z, r in zip(roots, rights)]
+    return [z * (1.0 / jnp.sqrt(norm)) for z, norm in zip(roots, norms)]
 
 
 def subspace_kernel(share, blocks, dofs, grams, *refs):
-    parts, (start, coef_out, energy_out) = refs[:grams], refs[grams:]
+    parts, (wide, tall, coef_out, energy_out) = refs[:grams], refs[grams:]
     value = parts[0][...]
     for part in parts[1:]:
         value = value + part[...]
     gram = spread_gram(value * (1.0 / dofs), share, blocks)
-    nxt = mm(gram, start[...])
+    freqs = range(share)
+    tall_next = mm(tall[...], gram)
+    images = [mm(gram, mm(gram, wide[f])) for f in freqs]
     for step in range(ITERS):
-        image = mm(gram, nxt)
-        root = inverse_root(mm(nxt, image, (0, 0)), share)
+        rows = [tall_next[f * WIDTH : (f + 1) * WIDTH] for f in freqs]
+        inners = [mm(rows[f], images[f]) for f in freqs]
         if step < ITERS - 1:
-            nxt = mm(image, root)
-    coef, image = mm(nxt, root), mm(image, root)
+            tall_image = mm(tall_next, gram)
+            ahead = [mm(gram, image) for image in images]
+        roots = inverse_roots(inners)
+        rights = [thirds(root) for root in roots]
+        if step < ITERS - 1:
+            tall_next = jnp.concatenate(
+                [
+                    packed_mm(roots[f], thirds(tall_image[f * WIDTH : (f + 1) * WIDTH]))
+                    for f in freqs
+                ],
+                0,
+            )
+            images = [packed_mm(ahead[f], rights[f]) for f in freqs]
     half = share * blocks
-    row, lane = iota(coef.shape, 0), iota(coef.shape, 1)
-    same = (row // half + lane // RANK) % 2 == 0
-    coef_out[...] = jnp.where(same, coef, -coef).astype(BF16)
-    energy = jnp.sum(image * image, axis=0, keepdims=True)
     me = lax.axis_index("blk")
     energy_out[...] = jnp.zeros_like(energy_out)
-    for f in range(share):
-        energy_out[pl.ds(me * share + f, 1), :] = energy[:, 2 * f * RANK : (2 * f + 1) * RANK]
+    for f in freqs:
+        final = packed_mm(images[f], rights[f])
+        energy = jnp.sum(final * final, axis=0, keepdims=True)
+        energy_out[pl.ds(me * share + f, 1), :] = energy[:, :RANK]
+    for f in freqs:
+        coef = packed_mm(roots[f], thirds(rows[f]))
+        same = (iota(coef.shape, 0) // RANK + iota(coef.shape, 1) // half) % 2 == 0
+        coef_out[f * WIDTH : (f + 1) * WIDTH] = jnp.where(same, coef, -coef).astype(BF16)
 
 
 def modes_kernel(share, quad, coef, *refs):
@@ -228,13 +271,9 @@
     points = quad.shape[-1]
     inverse = 1.0 / jnp.sqrt(quad[...])
     for c in range(data.shape[-1] // points):
-        modes = lax.dot_general(
-            coef[...],
-            data[:, c * points : (c + 1) * points],
-            (((0,), (0,)), ((), ())),
-            preferred_element_type=F32,
+        modes = inverse * jnp.dot(
+            coef[...], data[:, c * points : (c + 1) * points], preferred_element_type=F32
         )
-        modes = modes * inverse
         for f in range(share):
             for part in range(2):
                 at = (2 * f + part) * RANK
@@ -286,9 +325,12 @@
         ],
     )(in_hbm(snapshots.transpose(0, 2, 1, 3)), table, in_hbm(quad))
 
-    start = call(
+    wide, tall = call(
         functools.partial(start_kernel, share, blocks),
-        jax.ShapeDtypeStruct((size, 2 * share * RANK), F32),
+        [
+            jax.ShapeDtypeStruct((share, size, COPIES * WIDTH), F32),
+            jax.ShapeDtypeStruct((share * WIDTH, size), F32),
+        ],
         [HBM, pl.BlockSpec(memory_space=pl.ANY)],
         "start",
         [pltpu.VMEM((share, 2, RANK, groups * blocks), F32), pltpu.SemaphoreType.DMA],
@@ -298,6 +340,7 @@
     pieces[0] = spectra[0][0]
     arrived = {far: exchange(spectra[far], "blk", 2 * far) for far in range(reach - 1, 0, -1)}
     pieces[1] = exchange(spectra[0][1], "blk", 1)
+    wide, tall, arrived[1] = lax.optimization_barrier((wide, tall, arrived[1]))
     for far in range(reach - 1, 0, -1):
         pieces[2 * far] = arrived[far][0]
         pieces[2 * far + 1] = exchange(arrived[far][1], "blk", 1)
@@ -310,19 +353,19 @@
         "gram",
     )(*pieces)
     if spaces <= 4:
-        grams = [gram] + [exchange(gram, "space", d) for d in range(spaces - 1, 0, -1)]
+        grams = [gram] + [exchange(gram, "space", d) for d in range(1, spaces)]
     else:
         grams = [lax.psum(gram, "space")]
 
     coef, energies = call(
         functools.partial(subspace_kernel, share, blocks, width * spaces, len(grams)),
         [
-            jax.ShapeDtypeStruct((size, 2 * share * RANK), BF16),
+            jax.ShapeDtypeStruct((share * WIDTH, size), BF16),
             jax.ShapeDtypeStruct((NF, RANK), F32),
         ],
-        [VMEM] * (len(grams) + 1),
+        [VMEM] * (len(grams) + 2),
         "subspace",
-    )(*grams, start)
+    )(*grams, wide, tall)
 
     modes = call(
         functools.partial(modes_kernel, share),
@@ -332,7 +375,7 @@
     )(quad, coef, *pieces)
 
     energies = energies + exchange(energies, "blk", 1)
-    shares = [exchange(energies, "blk", 2 * far) for far in range(reach - 1, 0, -1)]
+    shares = [exchange(energies, "blk", 2 * far) for far in range(1, reach)]
     for other in shares:
         energies = energies + other
     return modes.transpose(0, 1, 3, 2, 4), energies

time: 49.7 us -> 45.5 us (0.915)
  waiting for transfers between devices: 15.5 us -> 13.3 us
  Pallas kernels: 17.8 us -> 15.9 us
    ppermute x14, waiting for transfers between devices: 15.5 us -> 13.3 us  [exchange(): return lax.ppermute(array, axis, [(i, i ^ distance) for i in range(size)])]
    pallas_call x1, Pallas kernels: 10.9 us -> 8.97 us  [per_device(): call(functools.partial(subspace_kernel, share, blocks, width * spaces, le...]
where the time goes in v1:
time: 45.5 us; the launch traced here: 45.2 us
  Pallas kernels  15.9 us (35%)
  starting transfers between devices  14.7 us (32%)
  waiting for transfers between devices  13.3 us (29%)
  between operations  0.73 us (2%)
  other arithmetic  0.61 us (1%)
    ppermute x14, starting transfers between devices, exchange(): return lax.ppermute(array, axis, [(i, i ^ distance) for i in range(size)])  14.7 us
    ppermute x14, waiting for transfers between devices, exchange(): return lax.ppermute(array, axis, [(i, i ^ distance) for i in range(size)])  13.3 us
    pallas_call x1, Pallas kernels, per_device(): call(functools.partial(subspace_kernel, share, blocks, width * spaces, le...  8.97 us
    pallas_call x1, Pallas kernels, per_device(): call(functools.partial(spectra_kernel, groups), [jax.ShapeDtypeStruct((2,...  4.07 us
    pallas_call x1, Pallas kernels, per_device(): call(functools.partial(start_kernel, share, blocks), [jax.ShapeDtypeStruc...  1.53 us
    pallas_call x1, Pallas kernels, per_device(): call(functools.partial(modes_kernel, share), jax.ShapeDtypeStruct((share,...  0.95 us
  transfers between devices with their start and end apart: 14, of which 9 were waited for; matrix products, arithmetic and copies ran while one was open for 0% of the time, Pallas kernels for 5%

profile of v1, /device:TPU:0, one launch (start us, length us, event | category | flops | bytes accessed | tf_op | source)
XLA Modules:
  0.0 45.2 jit_solution(1325937894575917660)
XLA Ops:
  0.6 0.0 copy-start
  0.6 4.1 %spectra.1 = (bf16[2,16,1536]{2,1,0:T(8,128)(2,1)S(1)}, bf16[2,16,1536]{2,1,0:T(8,128)(2,1)S(1)}, bf16[2,16,1536]{2,1,0:T(8,128)(2,1)S(1)}, bf16[2,16,1536]{2,1,0:T(8,128)(2,1)S(1)}) custom-call(bf16[4,3,512,512]{3,2,1,0:T(8,128)(2,1)} %bitcast.22, bf16[128,2048]{1,0:T(8,128)(2,1)} %constant.2.clone.table_hbm, f32[1,512]{1,0:T(1,128)} %bitcast.20), custom_call_target="tpu_custom_call" | custom-call | tf_op jit(solution)/shard_map/spectra/pallas_call | solution.py:313
  4.7 3.1 %collective-permute-start.1 = (bf16[2,16,1536]{2,1,0:T(8,128)(2,1)S(1)}, bf16[2,16,1536]{2,1,0:T(8,128)(2,1)S(1)}, u32[]{:S(2)}, u32[]{:S(2)}) collective-permute-start(bf16[2,16,1536]{2,1,0:T(8,128)(2,1)S(1)} %get-tuple-element.16), channel_id=1, source_target_pairs={{0,2},{1,3},{2,0},{3,1},{4,6},{5,7},{6,4},{7,5},{8,10},{9,11},{10,... | collective-permute-start | bytes 294920 | tf_op jit(solution)/shard_map/ppermute | solution.py:297
  7.8 0.1 collective-permute-start
  7.9 2.7 %collective-permute-start.3 = (bf16[2,16,1536]{2,1,0:T(8,128)(2,1)S(1)}, bf16[2,16,1536]{2,1,0:T(8,128)(2,1)S(1)}, u32[]{:S(2)}, u32[]{:S(2)}) collective-permute-start(bf16[2,16,1536]{2,1,0:T(8,128)(2,1)S(1)} %get-tuple-element.18), channel_id=1, source_target_pairs={{0,4},{1,5},{2,6},{3,7},{4,0},{5,1},{6,2},{7,3},{8,12},{9,13},{10,... | collective-permute-start | bytes 294920 | tf_op jit(solution)/shard_map/ppermute | solution.py:297
  10.5 0.0 collective-permute-start.5
  10.5 1.5 %start.1 = (f32[2,128,128]{2,1,0:T(8,128)S(1)}, f32[64,128]{1,0:T(8,128)S(1)}) custom-call(f32[16,2,16,32]{3,2,1,0:T(8,128)} %bitcast.24, bf16[2,16,1536]{2,1,0:T(8,128)(2,1)S(1)} %get-tuple-element.13._), custom_call_target="tpu_custom_call" | custom-call | tf_op jit(solution)/shard_map/start/pallas_call | solution.py:328
  12.1 0.0 collective-permute-done.1
  12.1 0.2 collective-permute-start.2
  12.3 6.0 %collective-permute-done.3 = bf16[2,16,1536]{2,1,0:T(8,128)(2,1)S(1)} collective-permute-done((bf16[2,16,1536]{2,1,0:T(8,128)(2,1)S(1)}, bf16[2,16,1536]{2,1,0:T(8,128)(2,1)S(1)}, u32[]{:S(2)}, u32[]{:S(2)}) %collective-permute-start.3) | collective-permute-done | bytes 98336 | tf_op jit(solution)/shard_map/ppermute | solution.py:297
  18.4 0.1 collective-permute-start.4
  18.4 0.0 collective-permute-done.5
  18.5 0.5 %collective-permute-start.6 = (bf16[16,1536]{1,0:T(8,128)(2,1)S(1)}, bf16[16,1536]{1,0:T(8,128)(2,1)S(1)}, u32[]{:S(2)}, u32[]{:S(2)}) collective-permute-start(bf16[16,1536]{1,0:T(8,128)(2,1)S(1)} %get-tuple-element.24), channel_id=1, source_target_pairs={{0,1},{1,0},{2,3},{3,2},{4,5},{5,4},{6,7},{7,6},{8,9},{9,8},{10,11... | collective-permute-start | bytes 147464 | tf_op jit(solution)/shard_map/ppermute | solution.py:297
  19.0 0.0 collective-permute-done.refs_1_
  19.0 0.0 collective-permute-done.2.refs_3_
  19.0 0.6 %collective-permute-done.4.refs_5_ = bf16[16,1536]{1,0:T(8,128)(2,1)S(1)} collective-permute-done((bf16[16,1536]{1,0:T(8,128)(2,1)S(1)}, bf16[16,1536]{1,0:T(8,128)(2,1)S(1)}, u32[]{:S(2)}, u32[]{:S(2)}) %collective-permute-start.4) | collective-permute-done | bytes 49184 | tf_op jit(solution)/shard_map/ppermute | solution.py:297
  19.7 0.2 collective-permute-done.6.refs_7_
  19.9 0.3 gram.1.refs_0_
  20.2 2.6 %collective-permute-start.9 = (f32[32,128]{1,0:T(8,128)S(1)}, f32[32,128]{1,0:T(8,128)S(1)}, u32[]{:S(2)}, u32[]{:S(2)}) collective-permute-start(f32[32,128]{1,0:T(8,128)S(1)} %gram.1.refs_0_), channel_id=1, source_target_pairs={{0,24},{8,16},{16,8},{24,0},{1,25},{9,17},{17,9},{25,1},{2,26},{10... | collective-permute-start | bytes 49160 | tf_op jit(solution)/shard_map/ppermute | solution.py:297
  22.8 0.5 %collective-permute-start.8 = (f32[32,128]{1,0:T(8,128)S(1)}, f32[32,128]{1,0:T(8,128)S(1)}, u32[]{:S(2)}, u32[]{:S(2)}) collective-permute-start(f32[32,128]{1,0:T(8,128)S(1)} %gram.1.refs_0_), channel_id=1, source_target_pairs={{0,16},{8,24},{16,0},{24,8},{1,17},{9,25},{17,1},{25,9},{2,18},{10... | collective-permute-start | bytes 49160 | tf_op jit(solution)/shard_map/ppermute | solution.py:297
  23.3 0.5 %collective-permute-start.7 = (f32[32,128]{1,0:T(8,128)S(1)}, f32[32,128]{1,0:T(8,128)S(1)}, u32[]{:S(2)}, u32[]{:S(2)}) collective-permute-start(f32[32,128]{1,0:T(8,128)S(1)} %gram.1.refs_0_), channel_id=1, source_target_pairs={{0,8},{8,0},{16,24},{24,16},{1,9},{9,1},{17,25},{25,17},{2,10},{10... | collective-permute-start | bytes 49160 | tf_op jit(solution)/shard_map/ppermute | solution.py:297
  23.8 1.1 %collective-permute-done.9.refs_3_ = f32[32,128]{1,0:T(8,128)S(1)} collective-permute-done((f32[32,128]{1,0:T(8,128)S(1)}, f32[32,128]{1,0:T(8,128)S(1)}, u32[]{:S(2)}, u32[]{:S(2)}) %collective-permute-start.9) | collective-permute-done | bytes 16416 | tf_op jit(solution)/shard_map/ppermute | solution.py:297
  24.9 1.6 %collective-permute-done.8.refs_2_ = f32[32,128]{1,0:T(8,128)S(1)} collective-permute-done((f32[32,128]{1,0:T(8,128)S(1)}, f32[32,128]{1,0:T(8,128)S(1)}, u32[]{:S(2)}, u32[]{:S(2)}) %collective-permute-start.8) | collective-permute-done | bytes 16416 | tf_op jit(solution)/shard_map/ppermute | solution.py:297
  26.5 0.5 %collective-permute-done.7.refs_1_ = f32[32,128]{1,0:T(8,128)S(1)} collective-permute-done((f32[32,128]{1,0:T(8,128)S(1)}, f32[32,128]{1,0:T(8,128)S(1)}, u32[]{:S(2)}, u32[]{:S(2)}) %collective-permute-start.7) | collective-permute-done | bytes 16416 | tf_op jit(solution)/shard_map/ppermute | solution.py:297
  27.0 9.0 %subspace.1 = (bf16[64,128]{1,0:T(8,128)(2,1)S(1)}, f32[16,16]{1,0:T(8,128)S(1)}) custom-call(f32[32,128]{1,0:T(8,128)S(1)} %gram.1.refs_0_, f32[32,128]{1,0:T(8,128)S(1)} %collective-permute-done.7.refs_1_, f32[32,128]{1,0:T(8,128)S(1)} %collective-permute-done.8.refs_2_, f32[32,128]{1,0:T(8,128)S(1)} %collective-permute-done.9.refs_3_, ...), custom_call_target="tpu_custom_call" | custom-call | tf_op jit(solution)/shard_map/subspace/pallas_call | solution.py:360
  36.0 0.1 collective-permute-start.10
  36.1 1.2 %collective-permute-done.10 = f32[16,16]{1,0:T(8,128)S(1)} collective-permute-done((f32[16,16]{1,0:T(8,128)S(1)}, f32[16,16]{1,0:T(8,128)S(1)}, u32[]{:S(2)}, u32[]{:S(2)}) %collective-permute-start.10) | collective-permute-done | bytes 1056 | tf_op jit(solution)/shard_map/ppermute | solution.py:297
  37.2 2.8 %collective-permute-start.13 = (f32[16,16]{1,0:T(8,128)S(1)}, f32[16,16]{1,0:T(8,128)S(1)}, u32[]{:S(2)}, u32[]{:S(2)}) collective-permute-start(f32[16,16]{1,0:T(8,128)S(1)} %add.12), channel_id=1, source_target_pairs={{0,6},{1,7},{2,4},{3,5},{4,2},{5,3},{6,0},{7,1},{8,14},{9,15},{10,... | collective-permute-start | bytes 3080 | tf_op jit(solution)/shard_map/ppermute | solution.py:297
  40.0 0.9 %collective-permute-start.12 = (f32[16,16]{1,0:T(8,128)S(1)}, f32[16,16]{1,0:T(8,128)S(1)}, u32[]{:S(2)}, u32[]{:S(2)}) collective-permute-start(f32[16,16]{1,0:T(8,128)S(1)} %add.12), channel_id=1, source_target_pairs={{0,4},{1,5},{2,6},{3,7},{4,0},{5,1},{6,2},{7,3},{8,12},{9,13},{10,... | collective-permute-start | bytes 3080 | tf_op jit(solution)/shard_map/ppermute | solution.py:297
  40.9 0.7 %collective-permute-start.11 = (f32[16,16]{1,0:T(8,128)S(1)}, f32[16,16]{1,0:T(8,128)S(1)}, u32[]{:S(2)}, u32[]{:S(2)}) collective-permute-start(f32[16,16]{1,0:T(8,128)S(1)} %add.12), channel_id=1, source_target_pairs={{0,2},{1,3},{2,0},{3,1},{4,6},{5,7},{6,4},{7,5},{8,10},{9,11},{10,... | collective-permute-start | bytes 3080 | tf_op jit(solution)/shard_map/ppermute | solution.py:297
  41.6 0.0 copy-done
  41.6 0.9 %modes.1 = f32[2,2,3,16,512]{4,3,2,1,0:T(8,128)} custom-call(f32[1,512]{1,0:T(1,128)S(1)} %bitcast.21, bf16[64,128]{1,0:T(8,128)(2,1)S(1)} %get-tuple-element.22.coef, bf16[16,1536]{1,0:T(8,128)(2,1)S(1)} %get-tuple-element.31.refs_0_, bf16[16,1536]{1,0:T(8,128)(2,1)S(1)} %collective-permute-done.refs_1_, bf16[16,1536]{1,0:T(8,128)(2,1)S(1)} %get-tuple-element.29.refs_2_, ...), custom_call_target="tpu_custom_call" | custom-call | tf_op jit(solution)/shard_map/modes/pallas_call | solution.py:370
  42.6 0.1 collective-permute-done.13
  42.7 1.9 %collective-permute-done.12 = f32[16,16]{1,0:T(8,128)S(1)} collective-permute-done((f32[16,16]{1,0:T(8,128)S(1)}, f32[16,16]{1,0:T(8,128)S(1)}, u32[]{:S(2)}, u32[]{:S(2)}) %collective-permute-start.12) | collective-permute-done | bytes 1056 | tf_op jit(solution)/shard_map/ppermute | solution.py:297
  44.6 0.0 collective-permute-done.11
  44.6 0.6 %add_add_fusion = f32[16,16]{1,0:T(8,128)} fusion(f32[16,16]{1,0:T(8,128)S(1)} %collective-permute-done.13, f32[16,16]{1,0:T(8,128)S(1)} %collective-permute-done.12, f32[16,16]{1,0:T(8,128)S(1)} %add.12, f32[16,16]{1,0:T(8,128)S(1)} %collective-permute-done.11), kind=kLoop, calls=%fused_computation.8 | loop fusion | flops 768 | bytes 5120 | tf_op jit(solution)/shard_map/add | solution.py:380
  (5 shorter events, 0.0 us)
Async XLA Ops:
  0.6 41.0 %copy-start = (f32[512]{0:T(512)S(1)}, f32[512]{0:T(512)}, u32[]{:S(2)}) copy-start(f32[512]{0:T(512)} %param.5) | copy-start | bytes 6148
  4.7 7.4 %collective-permute-start.1 = (bf16[2,16,1536]{2,1,0:T(8,128)(2,1)S(1)}, bf16[2,16,1536]{2,1,0:T(8,128)(2,1)S(1)}, u32[]{:S(2)}, u32[]{:S(2)}) collective-permute-start(bf16[2,16,1536]{2,1,0:T(8,128)(2,1)S(1)} %get-tuple-element.16), channel_id=1, source_target_pairs={{0,2},{1,3},{2,0},{3,1},{4,6},{5,7},{6,4},{7,5},{8,10},{9,11},{10,... | collective-permute-start | bytes 294920 | tf_op jit(solution)/shard_map/ppermute | solution.py:297
  7.8 11.2 %collective-permute-start = (bf16[16,1536]{1,0:T(8,128)(2,1)S(1)}, bf16[16,1536]{1,0:T(8,128)(2,1)S(1)}, u32[]{:S(2)}, u32[]{:S(2)}) collective-permute-start(bf16[16,1536]{1,0:T(8,128)(2,1)S(1)} %get-tuple-element.30), channel_id=1, source_target_pairs={{0,1},{1,0},{2,3},{3,2},{4,5},{5,4},{6,7},{7,6},{8,9},{9,8},{10,11... | collective-permute-start | bytes 147464 | tf_op jit(solution)/shard_map/ppermute | solution.py:297
  7.9 10.5 %collective-permute-start.3 = (bf16[2,16,1536]{2,1,0:T(8,128)(2,1)S(1)}, bf16[2,16,1536]{2,1,0:T(8,128)(2,1)S(1)}, u32[]{:S(2)}, u32[]{:S(2)}) collective-permute-start(bf16[2,16,1536]{2,1,0:T(8,128)(2,1)S(1)} %get-tuple-element.18), channel_id=1, source_target_pairs={{0,4},{1,5},{2,6},{3,7},{4,0},{5,1},{6,2},{7,3},{8,12},{9,13},{10,... | collective-permute-start | bytes 294920 | tf_op jit(solution)/shard_map/ppermute | solution.py:297
  10.5 7.9 %collective-permute-start.5 = (bf16[2,16,1536]{2,1,0:T(8,128)(2,1)S(1)}, bf16[2,16,1536]{2,1,0:T(8,128)(2,1)S(1)}, u32[]{:S(2)}, u32[]{:S(2)}) collective-permute-start(bf16[2,16,1536]{2,1,0:T(8,128)(2,1)S(1)} %get-tuple-element.19), channel_id=1, source_target_pairs={{0,6},{1,7},{2,4},{3,5},{4,2},{5,3},{6,0},{7,1},{8,14},{9,15},{10,... | collective-permute-start | bytes 294920 | tf_op jit(solution)/shard_map/ppermute | solution.py:297
  12.1 6.9 %collective-permute-start.2 = (bf16[16,1536]{1,0:T(8,128)(2,1)S(1)}, bf16[16,1536]{1,0:T(8,128)(2,1)S(1)}, u32[]{:S(2)}, u32[]{:S(2)}) collective-permute-start(bf16[16,1536]{1,0:T(8,128)(2,1)S(1)} %get-tuple-element.28), channel_id=1, source_target_pairs={{0,1},{1,0},{2,3},{3,2},{4,5},{5,4},{6,7},{7,6},{8,9},{9,8},{10,11... | collective-permute-start | bytes 147464 | tf_op jit(solution)/shard_map/ppermute | solution.py:297
  18.4 1.3 %collective-permute-start.4 = (bf16[16,1536]{1,0:T(8,128)(2,1)S(1)}, bf16[16,1536]{1,0:T(8,128)(2,1)S(1)}, u32[]{:S(2)}, u32[]{:S(2)}) collective-permute-start(bf16[16,1536]{1,0:T(8,128)(2,1)S(1)} %get-tuple-element.26), channel_id=1, source_target_pairs={{0,1},{1,0},{2,3},{3,2},{4,5},{5,4},{6,7},{7,6},{8,9},{9,8},{10,11... | collective-permute-start | bytes 147464 | tf_op jit(solution)/shard_map/ppermute | solution.py:297
  18.5 1.4 %collective-permute-start.6 = (bf16[16,1536]{1,0:T(8,128)(2,1)S(1)}, bf16[16,1536]{1,0:T(8,128)(2,1)S(1)}, u32[]{:S(2)}, u32[]{:S(2)}) collective-permute-start(bf16[16,1536]{1,0:T(8,128)(2,1)S(1)} %get-tuple-element.24), channel_id=1, source_target_pairs={{0,1},{1,0},{2,3},{3,2},{4,5},{5,4},{6,7},{7,6},{8,9},{9,8},{10,11... | collective-permute-start | bytes 147464 | tf_op jit(solution)/shard_map/ppermute | solution.py:297
  20.2 4.7 %collective-permute-start.9 = (f32[32,128]{1,0:T(8,128)S(1)}, f32[32,128]{1,0:T(8,128)S(1)}, u32[]{:S(2)}, u32[]{:S(2)}) collective-permute-start(f32[32,128]{1,0:T(8,128)S(1)} %gram.1.refs_0_), channel_id=1, source_target_pairs={{0,24},{8,16},{16,8},{24,0},{1,25},{9,17},{17,9},{25,1},{2,26},{10... | collective-permute-start | bytes 49160 | tf_op jit(solution)/shard_map/ppermute | solution.py:297
  22.8 3.7 %collective-permute-start.8 = (f32[32,128]{1,0:T(8,128)S(1)}, f32[32,128]{1,0:T(8,128)S(1)}, u32[]{:S(2)}, u32[]{:S(2)}) collective-permute-start(f32[32,128]{1,0:T(8,128)S(1)} %gram.1.refs_0_), channel_id=1, source_target_pairs={{0,16},{8,24},{16,0},{24,8},{1,17},{9,25},{17,1},{25,9},{2,18},{10... | collective-permute-start | bytes 49160 | tf_op jit(solution)/shard_map/ppermute | solution.py:297
  23.3 3.7 %collective-permute-start.7 = (f32[32,128]{1,0:T(8,128)S(1)}, f32[32,128]{1,0:T(8,128)S(1)}, u32[]{:S(2)}, u32[]{:S(2)}) collective-permute-start(f32[32,128]{1,0:T(8,128)S(1)} %gram.1.refs_0_), channel_id=1, source_target_pairs={{0,8},{8,0},{16,24},{24,16},{1,9},{9,1},{17,25},{25,17},{2,10},{10... | collective-permute-start | bytes 49160 | tf_op jit(solution)/shard_map/ppermute | solution.py:297
  36.0 1.2 %collective-permute-start.10 = (f32[16,16]{1,0:T(8,128)S(1)}, f32[16,16]{1,0:T(8,128)S(1)}, u32[]{:S(2)}, u32[]{:S(2)}) collective-permute-start(f32[16,16]{1,0:T(8,128)S(1)} %get-tuple-element.23), channel_id=1, source_target_pairs={{0,1},{1,0},{2,3},{3,2},{4,5},{5,4},{6,7},{7,6},{8,9},{9,8},{10,11... | collective-permute-start | bytes 3080 | tf_op jit(solution)/shard_map/ppermute | solution.py:297
  37.2 5.4 %collective-permute-start.13 = (f32[16,16]{1,0:T(8,128)S(1)}, f32[16,16]{1,0:T(8,128)S(1)}, u32[]{:S(2)}, u32[]{:S(2)}) collective-permute-start(f32[16,16]{1,0:T(8,128)S(1)} %add.12), channel_id=1, source_target_pairs={{0,6},{1,7},{2,4},{3,5},{4,2},{5,3},{6,0},{7,1},{8,14},{9,15},{10,... | collective-permute-start | bytes 3080 | tf_op jit(solution)/shard_map/ppermute | solution.py:297
  40.0 4.6 %collective-permute-start.12 = (f32[16,16]{1,0:T(8,128)S(1)}, f32[16,16]{1,0:T(8,128)S(1)}, u32[]{:S(2)}, u32[]{:S(2)}) collective-permute-start(f32[16,16]{1,0:T(8,128)S(1)} %add.12), channel_id=1, source_target_pairs={{0,4},{1,5},{2,6},{3,7},{4,0},{5,1},{6,2},{7,3},{8,12},{9,13},{10,... | collective-permute-start | bytes 3080 | tf_op jit(solution)/shard_map/ppermute | solution.py:297
  40.9 3.7 %collective-permute-start.11 = (f32[16,16]{1,0:T(8,128)S(1)}, f32[16,16]{1,0:T(8,128)S(1)}, u32[]{:S(2)}, u32[]{:S(2)}) collective-permute-start(f32[16,16]{1,0:T(8,128)S(1)} %add.12), channel_id=1, source_target_pairs={{0,2},{1,3},{2,0},{3,1},{4,6},{5,7},{6,4},{7,5},{8,10},{9,11},{10,... | collective-permute-start | bytes 3080 | tf_op jit(solution)/shard_map/ppermute | solution.py:297

commit v2 on v1

--- a/solution.py
+++ b/solution.py
@@ -17,7 +17,7 @@
 FULL_STEPS = 6
 WIDTH = 2 * RANK
 COPIES = 4
-IN_FLIGHT = 6
+IN_FLIGHT = 8
 LIMIT = 40 * 2**20
 F32, BF16 = jnp.float32, jnp.bfloat16
 HBM = pl.BlockSpec(memory_space=pltpu.HBM)
@@ -336,14 +336,11 @@
         [pltpu.VMEM((share, 2, RANK, groups * blocks), F32), pltpu.SemaphoreType.DMA],
     )(in_hbm(omega.transpose(0, 1, 3, 2)), spectra[0])
 
-    pieces = [None] * groups
-    pieces[0] = spectra[0][0]
     arrived = {far: exchange(spectra[far], "blk", 2 * far) for far in range(reach - 1, 0, -1)}
-    pieces[1] = exchange(spectra[0][1], "blk", 1)
-    wide, tall, arrived[1] = lax.optimization_barrier((wide, tall, arrived[1]))
-    for far in range(reach - 1, 0, -1):
-        pieces[2 * far] = arrived[far][0]
-        pieces[2 * far + 1] = exchange(arrived[far][1], "blk", 1)
+    wide, tall, arrived = lax.optimization_barrier((wide, tall, arrived))
+    arrived[0] = spectra[0]
+    sent = exchange(jnp.stack([arrived[far][1] for far in range(reach)]), "blk", 1)
+    pieces = [piece for far in range(reach) for piece in (arrived[far][0], sent[far])]
 
     packed = (size * (blocks if share * blocks == 8 else height) // height, size)
     gram = call(

time: 45.5 us -> 44.9 us (0.987)
  starting transfers between devices: 14.7 us -> 13.8 us
    ppermute x14 -> x11, starting transfers between devices: 14.7 us -> 13.8 us  [exchange(): return lax.ppermute(array, axis, [(i, i ^ distance) for i in range(size)])]
    ppermute x14 -> x11, waiting for transfers between devices: 13.3 us -> 13.7 us  [exchange(): return lax.ppermute(array, axis, [(i, i ^ distance) for i in range(size)])]
  transfers between devices with their start and end apart: 14 -> 11, of which waited for: 9 -> 8; matrix products, arithmetic and copies ran while one was open for 0% -> 0% of each run, Pallas kernels for 5% -> 6%
where the time goes in v2:
time: 44.9 us; the launch traced here: 44.7 us
  Pallas kernels  15.8 us (35%)
  starting transfers between devices  13.8 us (31%)
  waiting for transfers between devices  13.7 us (31%)
  between operations  0.72 us (2%)
  other arithmetic  0.64 us (1%)
    ppermute x11, starting transfers between devices, exchange(): return lax.ppermute(array, axis, [(i, i ^ distance) for i in range(size)])  13.8 us
    ppermute x11, waiting for transfers between devices, exchange(): return lax.ppermute(array, axis, [(i, i ^ distance) for i in range(size)])  13.7 us
    pallas_call x1, Pallas kernels, per_device(): call(functools.partial(subspace_kernel, share, blocks, width * spaces, le...  8.97 us
    pallas_call x1, Pallas kernels, per_device(): call(functools.partial(spectra_kernel, groups), [jax.ShapeDtypeStruct((2,...  4.02 us
    pallas_call x1, Pallas kernels, per_device(): call(functools.partial(start_kernel, share, blocks), [jax.ShapeDtypeStruc...  1.54 us
    pallas_call x1, Pallas kernels, per_device(): call(functools.partial(modes_kernel, share), jax.ShapeDtypeStruct((share,...  0.95 us
  transfers between devices with their start and end apart: 11, of which 8 were waited for; matrix products, arithmetic and copies ran while one was open for 0% of the time, Pallas kernels for 6%

profile of v2, /device:TPU:0, one launch (start us, length us, event | category | flops | bytes accessed | tf_op | source)
XLA Modules:
  0.0 44.7 jit_solution(7194373197615811635)
XLA Ops:
  0.6 0.0 copy-start
  0.6 4.0 %spectra.1 = (bf16[2,16,1536]{2,1,0:T(8,128)(2,1)S(1)}, bf16[2,16,1536]{2,1,0:T(8,128)(2,1)S(1)}, bf16[2,16,1536]{2,1,0:T(8,128)(2,1)S(1)}, bf16[2,16,1536]{2,1,0:T(8,128)(2,1)S(1)}) custom-call(bf16[4,3,512,512]{3,2,1,0:T(8,128)(2,1)} %bitcast.22, bf16[128,2048]{1,0:T(8,128)(2,1)} %constant.2.clone.table_hbm, f32[1,512]{1,0:T(1,128)} %bitcast.20), custom_call_target="tpu_custom_call" | custom-call | tf_op jit(solution)/shard_map/spectra/pallas_call | solution.py:313
  4.7 3.1 %collective-permute-start = (bf16[2,16,1536]{2,1,0:T(8,128)(2,1)S(1)}, bf16[2,16,1536]{2,1,0:T(8,128)(2,1)S(1)}, u32[]{:S(2)}, u32[]{:S(2)}) collective-permute-start(bf16[2,16,1536]{2,1,0:T(8,128)(2,1)S(1)} %get-tuple-element.18), channel_id=1, source_target_pairs={{0,2},{1,3},{2,0},{3,1},{4,6},{5,7},{6,4},{7,5},{8,10},{9,11},{10,... | collective-permute-start | bytes 294920 | tf_op jit(solution)/shard_map/ppermute | solution.py:297
  7.8 2.6 %collective-permute-start.1 = (bf16[2,16,1536]{2,1,0:T(8,128)(2,1)S(1)}, bf16[2,16,1536]{2,1,0:T(8,128)(2,1)S(1)}, u32[]{:S(2)}, u32[]{:S(2)}) collective-permute-start(bf16[2,16,1536]{2,1,0:T(8,128)(2,1)S(1)} %get-tuple-element.19), channel_id=1, source_target_pairs={{0,4},{1,5},{2,6},{3,7},{4,0},{5,1},{6,2},{7,3},{8,12},{9,13},{10,... | collective-permute-start | bytes 294920 | tf_op jit(solution)/shard_map/ppermute | solution.py:297
  10.3 0.0 collective-permute-start.2
  10.4 1.5 %start.1 = (f32[2,128,128]{2,1,0:T(8,128)S(1)}, f32[64,128]{1,0:T(8,128)S(1)}) custom-call(f32[16,2,16,32]{3,2,1,0:T(8,128)} %bitcast.24, bf16[2,16,1536]{2,1,0:T(8,128)(2,1)S(1)} %get-tuple-element.15._), custom_call_target="tpu_custom_call" | custom-call | tf_op jit(solution)/shard_map/start/pallas_call | solution.py:328
  11.9 0.0 collective-permute-done
  11.9 6.3 %collective-permute-done.1 = bf16[2,16,1536]{2,1,0:T(8,128)(2,1)S(1)} collective-permute-done((bf16[2,16,1536]{2,1,0:T(8,128)(2,1)S(1)}, bf16[2,16,1536]{2,1,0:T(8,128)(2,1)S(1)}, u32[]{:S(2)}, u32[]{:S(2)}) %collective-permute-start.1) | collective-permute-done | bytes 98336 | tf_op jit(solution)/shard_map/ppermute | solution.py:297
  18.2 0.0 collective-permute-done.2
  18.3 0.1 collective-permute-start.3
  18.3 1.4 %collective-permute-done.3 = bf16[4,16,1536]{2,1,0:T(8,128)(2,1)S(1)} collective-permute-done((bf16[4,16,1536]{2,1,0:T(8,128)(2,1)S(1)}, bf16[4,16,1536]{2,1,0:T(8,128)(2,1)S(1)}, u32[]{:S(2)}, u32[]{:S(2)}) %collective-permute-start.3) | collective-permute-done | bytes 196640 | tf_op jit(solution)/shard_map/ppermute | solution.py:297
  19.8 0.3 gram.1.refs_0_
  20.1 2.5 %collective-permute-start.6 = (f32[32,128]{1,0:T(8,128)S(1)}, f32[32,128]{1,0:T(8,128)S(1)}, u32[]{:S(2)}, u32[]{:S(2)}) collective-permute-start(f32[32,128]{1,0:T(8,128)S(1)} %gram.1.refs_0_), channel_id=1, source_target_pairs={{0,24},{8,16},{16,8},{24,0},{1,25},{9,17},{17,9},{25,1},{2,26},{10... | collective-permute-start | bytes 49160 | tf_op jit(solution)/shard_map/ppermute | solution.py:297
  22.6 0.5 %collective-permute-start.5 = (f32[32,128]{1,0:T(8,128)S(1)}, f32[32,128]{1,0:T(8,128)S(1)}, u32[]{:S(2)}, u32[]{:S(2)}) collective-permute-start(f32[32,128]{1,0:T(8,128)S(1)} %gram.1.refs_0_), channel_id=1, source_target_pairs={{0,16},{8,24},{16,0},{24,8},{1,17},{9,25},{17,1},{25,9},{2,18},{10... | collective-permute-start | bytes 49160 | tf_op jit(solution)/shard_map/ppermute | solution.py:297
  23.1 0.5 %collective-permute-start.4 = (f32[32,128]{1,0:T(8,128)S(1)}, f32[32,128]{1,0:T(8,128)S(1)}, u32[]{:S(2)}, u32[]{:S(2)}) collective-permute-start(f32[32,128]{1,0:T(8,128)S(1)} %gram.1.refs_0_), channel_id=1, source_target_pairs={{0,8},{8,0},{16,24},{24,16},{1,9},{9,1},{17,25},{25,17},{2,10},{10... | collective-permute-start | bytes 49160 | tf_op jit(solution)/shard_map/ppermute | solution.py:297
  23.7 1.1 %collective-permute-done.6.refs_3_ = f32[32,128]{1,0:T(8,128)S(1)} collective-permute-done((f32[32,128]{1,0:T(8,128)S(1)}, f32[32,128]{1,0:T(8,128)S(1)}, u32[]{:S(2)}, u32[]{:S(2)}) %collective-permute-start.6) | collective-permute-done | bytes 16416 | tf_op jit(solution)/shard_map/ppermute | solution.py:297
  24.8 1.5 %collective-permute-done.5.refs_2_ = f32[32,128]{1,0:T(8,128)S(1)} collective-permute-done((f32[32,128]{1,0:T(8,128)S(1)}, f32[32,128]{1,0:T(8,128)S(1)}, u32[]{:S(2)}, u32[]{:S(2)}) %collective-permute-start.5) | collective-permute-done | bytes 16416 | tf_op jit(solution)/shard_map/ppermute | solution.py:297
  26.4 0.5 %collective-permute-done.4.refs_1_ = f32[32,128]{1,0:T(8,128)S(1)} collective-permute-done((f32[32,128]{1,0:T(8,128)S(1)}, f32[32,128]{1,0:T(8,128)S(1)}, u32[]{:S(2)}, u32[]{:S(2)}) %collective-permute-start.4) | collective-permute-done | bytes 16416 | tf_op jit(solution)/shard_map/ppermute | solution.py:297
  26.9 9.0 %subspace.1 = (bf16[64,128]{1,0:T(8,128)(2,1)S(1)}, f32[16,16]{1,0:T(8,128)S(1)}) custom-call(f32[32,128]{1,0:T(8,128)S(1)} %gram.1.refs_0_, f32[32,128]{1,0:T(8,128)S(1)} %collective-permute-done.4.refs_1_, f32[32,128]{1,0:T(8,128)S(1)} %collective-permute-done.5.refs_2_, f32[32,128]{1,0:T(8,128)S(1)} %collective-permute-done.6.refs_3_, ...), custom_call_target="tpu_custom_call" | custom-call | tf_op jit(solution)/shard_map/subspace/pallas_call | solution.py:357
  35.9 0.1 collective-permute-start.7
  35.9 1.2 %collective-permute-done.7 = f32[16,16]{1,0:T(8,128)S(1)} collective-permute-done((f32[16,16]{1,0:T(8,128)S(1)}, f32[16,16]{1,0:T(8,128)S(1)}, u32[]{:S(2)}, u32[]{:S(2)}) %collective-permute-start.7) | collective-permute-done | bytes 1056 | tf_op jit(solution)/shard_map/ppermute | solution.py:297
  37.1 2.5 %collective-permute-start.10 = (f32[16,16]{1,0:T(8,128)S(1)}, f32[16,16]{1,0:T(8,128)S(1)}, u32[]{:S(2)}, u32[]{:S(2)}) collective-permute-start(f32[16,16]{1,0:T(8,128)S(1)} %add.12), channel_id=1, source_target_pairs={{0,6},{1,7},{2,4},{3,5},{4,2},{5,3},{6,0},{7,1},{8,14},{9,15},{10,... | collective-permute-start | bytes 3080 | tf_op jit(solution)/shard_map/ppermute | solution.py:297
  39.6 0.6 %collective-permute-start.9 = (f32[16,16]{1,0:T(8,128)S(1)}, f32[16,16]{1,0:T(8,128)S(1)}, u32[]{:S(2)}, u32[]{:S(2)}) collective-permute-start(f32[16,16]{1,0:T(8,128)S(1)} %add.12), channel_id=1, source_target_pairs={{0,4},{1,5},{2,6},{3,7},{4,0},{5,1},{6,2},{7,3},{8,12},{9,13},{10,... | collective-permute-start | bytes 3080 | tf_op jit(solution)/shard_map/ppermute | solution.py:297
  40.2 1.3 %collective-permute-start.8 = (f32[16,16]{1,0:T(8,128)S(1)}, f32[16,16]{1,0:T(8,128)S(1)}, u32[]{:S(2)}, u32[]{:S(2)}) collective-permute-start(f32[16,16]{1,0:T(8,128)S(1)} %add.12), channel_id=1, source_target_pairs={{0,2},{1,3},{2,0},{3,1},{4,6},{5,7},{6,4},{7,5},{8,10},{9,11},{10,... | collective-permute-start | bytes 3080 | tf_op jit(solution)/shard_map/ppermute | solution.py:297
  41.5 0.0 copy-done
  41.5 0.9 %modes.1 = f32[2,2,3,16,512]{4,3,2,1,0:T(8,128)} custom-call(f32[1,512]{1,0:T(1,128)S(1)} %bitcast.21, bf16[64,128]{1,0:T(8,128)(2,1)S(1)} %get-tuple-element.26.coef, bf16[16,1536]{1,0:T(8,128)(2,1)S(1)} %get-tuple-element.39.refs_0_, bf16[16,1536]{1,0:T(8,128)(2,1)S(1)} %get-tuple-element.31.refs_1_, bf16[16,1536]{1,0:T(8,128)(2,1)S(1)} %get-tuple-element.36.refs_2_, ...), custom_call_target="tpu_custom_call" | custom-call | tf_op jit(solution)/shard_map/modes/pallas_call | solution.py:367
  42.4 0.1 collective-permute-done.10
  42.5 1.6 %collective-permute-done.9 = f32[16,16]{1,0:T(8,128)S(1)} collective-permute-done((f32[16,16]{1,0:T(8,128)S(1)}, f32[16,16]{1,0:T(8,128)S(1)}, u32[]{:S(2)}, u32[]{:S(2)}) %collective-permute-start.9) | collective-permute-done | bytes 1056 | tf_op jit(solution)/shard_map/ppermute | solution.py:297
  44.1 0.0 collective-permute-done.8
  44.1 0.6 %add_add_fusion = f32[16,16]{1,0:T(8,128)} fusion(f32[16,16]{1,0:T(8,128)S(1)} %collective-permute-done.10, f32[16,16]{1,0:T(8,128)S(1)} %collective-permute-done.9, f32[16,16]{1,0:T(8,128)S(1)} %add.12, f32[16,16]{1,0:T(8,128)S(1)} %collective-permute-done.8), kind=kLoop, calls=%fused_computation.9 | loop fusion | flops 768 | bytes 5120 | tf_op jit(solution)/shard_map/add | solution.py:377
  (6 shorter events, 0.1 us)
Async XLA Ops:
  0.6 40.9 %copy-start = (f32[512]{0:T(512)S(1)}, f32[512]{0:T(512)}, u32[]{:S(2)}) copy-start(f32[512]{0:T(512)} %param.5) | copy-start | bytes 6148
  4.7 7.2 %collective-permute-start = (bf16[2,16,1536]{2,1,0:T(8,128)(2,1)S(1)}, bf16[2,16,1536]{2,1,0:T(8,128)(2,1)S(1)}, u32[]{:S(2)}, u32[]{:S(2)}) collective-permute-start(bf16[2,16,1536]{2,1,0:T(8,128)(2,1)S(1)} %get-tuple-element.18), channel_id=1, source_target_pairs={{0,2},{1,3},{2,0},{3,1},{4,6},{5,7},{6,4},{7,5},{8,10},{9,11},{10,... | collective-permute-start | bytes 294920 | tf_op jit(solution)/shard_map/ppermute | solution.py:297
  7.8 10.4 %collective-permute-start.1 = (bf16[2,16,1536]{2,1,0:T(8,128)(2,1)S(1)}, bf16[2,16,1536]{2,1,0:T(8,128)(2,1)S(1)}, u32[]{:S(2)}, u32[]{:S(2)}) collective-permute-start(bf16[2,16,1536]{2,1,0:T(8,128)(2,1)S(1)} %get-tuple-element.19), channel_id=1, source_target_pairs={{0,4},{1,5},{2,6},{3,7},{4,0},{5,1},{6,2},{7,3},{8,12},{9,13},{10,... | collective-permute-start | bytes 294920 | tf_op jit(solution)/shard_map/ppermute | solution.py:297
  10.3 7.8 %collective-permute-start.2 = (bf16[2,16,1536]{2,1,0:T(8,128)(2,1)S(1)}, bf16[2,16,1536]{2,1,0:T(8,128)(2,1)S(1)}, u32[]{:S(2)}, u32[]{:S(2)}) collective-permute-start(bf16[2,16,1536]{2,1,0:T(8,128)(2,1)S(1)} %get-tuple-element.20), channel_id=1, source_target_pairs={{0,6},{1,7},{2,4},{3,5},{4,2},{5,3},{6,0},{7,1},{8,14},{9,15},{10,... | collective-permute-start | bytes 294920 | tf_op jit(solution)/shard_map/ppermute | solution.py:297
  18.3 1.5 %collective-permute-start.3 = (bf16[4,16,1536]{2,1,0:T(8,128)(2,1)S(1)}, bf16[4,16,1536]{2,1,0:T(8,128)(2,1)S(1)}, u32[]{:S(2)}, u32[]{:S(2)}) collective-permute-start(bf16[4,16,1536]{2,1,0:T(8,128)(2,1)S(1)} %pad_maximum_fusion), channel_id=1, source_target_pairs={{0,1},{1,0},{2,3},{3,2},{4,5},{5,4},{6,7},{7,6},{8,9},{9,8},{10,11... | collective-permute-start | bytes 589832 | tf_op jit(solution)/shard_map/ppermute | solution.py:297
  20.1 4.7 %collective-permute-start.6 = (f32[32,128]{1,0:T(8,128)S(1)}, f32[32,128]{1,0:T(8,128)S(1)}, u32[]{:S(2)}, u32[]{:S(2)}) collective-permute-start(f32[32,128]{1,0:T(8,128)S(1)} %gram.1.refs_0_), channel_id=1, source_target_pairs={{0,24},{8,16},{16,8},{24,0},{1,25},{9,17},{17,9},{25,1},{2,26},{10... | collective-permute-start | bytes 49160 | tf_op jit(solution)/shard_map/ppermute | solution.py:297
  22.6 3.7 %collective-permute-start.5 = (f32[32,128]{1,0:T(8,128)S(1)}, f32[32,128]{1,0:T(8,128)S(1)}, u32[]{:S(2)}, u32[]{:S(2)}) collective-permute-start(f32[32,128]{1,0:T(8,128)S(1)} %gram.1.refs_0_), channel_id=1, source_target_pairs={{0,16},{8,24},{16,0},{24,8},{1,17},{9,25},{17,1},{25,9},{2,18},{10... | collective-permute-start | bytes 49160 | tf_op jit(solution)/shard_map/ppermute | solution.py:297
  23.1 3.7 %collective-permute-start.4 = (f32[32,128]{1,0:T(8,128)S(1)}, f32[32,128]{1,0:T(8,128)S(1)}, u32[]{:S(2)}, u32[]{:S(2)}) collective-permute-start(f32[32,128]{1,0:T(8,128)S(1)} %gram.1.refs_0_), channel_id=1, source_target_pairs={{0,8},{8,0},{16,24},{24,16},{1,9},{9,1},{17,25},{25,17},{2,10},{10... | collective-permute-start | bytes 49160 | tf_op jit(solution)/shard_map/ppermute | solution.py:297
  35.9 1.2 %collective-permute-start.7 = (f32[16,16]{1,0:T(8,128)S(1)}, f32[16,16]{1,0:T(8,128)S(1)}, u32[]{:S(2)}, u32[]{:S(2)}) collective-permute-start(f32[16,16]{1,0:T(8,128)S(1)} %get-tuple-element.27), channel_id=1, source_target_pairs={{0,1},{1,0},{2,3},{3,2},{4,5},{5,4},{6,7},{7,6},{8,9},{9,8},{10,11... | collective-permute-start | bytes 3080 | tf_op jit(solution)/shard_map/ppermute | solution.py:297
  37.1 5.4 %collective-permute-start.10 = (f32[16,16]{1,0:T(8,128)S(1)}, f32[16,16]{1,0:T(8,128)S(1)}, u32[]{:S(2)}, u32[]{:S(2)}) collective-permute-start(f32[16,16]{1,0:T(8,128)S(1)} %add.12), channel_id=1, source_target_pairs={{0,6},{1,7},{2,4},{3,5},{4,2},{5,3},{6,0},{7,1},{8,14},{9,15},{10,... | collective-permute-start | bytes 3080 | tf_op jit(solution)/shard_map/ppermute | solution.py:297
  39.6 4.5 %collective-permute-start.9 = (f32[16,16]{1,0:T(8,128)S(1)}, f32[16,16]{1,0:T(8,128)S(1)}, u32[]{:S(2)}, u32[]{:S(2)}) collective-permute-start(f32[16,16]{1,0:T(8,128)S(1)} %add.12), channel_id=1, source_target_pairs={{0,4},{1,5},{2,6},{3,7},{4,0},{5,1},{6,2},{7,3},{8,12},{9,13},{10,... | collective-permute-start | bytes 3080 | tf_op jit(solution)/shard_map/ppermute | solution.py:297
  40.2 4.0 %collective-permute-start.8 = (f32[16,16]{1,0:T(8,128)S(1)}, f32[16,16]{1,0:T(8,128)S(1)}, u32[]{:S(2)}, u32[]{:S(2)}) collective-permute-start(f32[16,16]{1,0:T(8,128)S(1)} %add.12), channel_id=1, source_target_pairs={{0,2},{1,3},{2,0},{3,1},{4,6},{5,7},{6,4},{7,5},{8,10},{9,11},{10,... | collective-permute-start | bytes 3080 | tf_op jit(solution)/shard_map/ppermute | solution.py:297

commit v3 on v2

--- a/solution.py
+++ b/solution.py
@@ -40,13 +40,10 @@
     return np.stack([window * np.cos(phases) * factor, -window * np.sin(phases) * factor])
 
 
-def wide_table(sample_count, groups, blocks):
-    share = NF // groups
-    rows = dft_table(sample_count, NF).reshape(2, groups, share, sample_count).transpose(1, 0, 2, 3)
-    wide = np.zeros((groups, 2, share, blocks, blocks, sample_count), np.float32)
-    for block in range(blocks):
-        wide[:, :, :, block, block] = rows
-    return wide.reshape(2 * NF * blocks, blocks * sample_count).astype(ml_dtypes.bfloat16)
+def table_rows(sample_count, groups):
+    rows = dft_table(sample_count, NF).reshape(2, groups, NF // groups, sample_count)
+    rows = rows.transpose(1, 0, 2, 3).reshape(2 * NF, sample_count)
+    return rows.astype(ml_dtypes.bfloat16)
 
 
 def iota(shape, axis):
@@ -61,24 +58,31 @@
 
 
 def spectra_kernel(groups, snap, table_hbm, quad_hbm, *refs):
-    outs, (buf, table, quad, piles, sems, small) = refs[:-6], refs[-6:]
+    outs, (buf, thin, quad, table, piles, sems, small) = refs[:-7], refs[-7:]
     blocks, comps, samples, points = snap.shape
     steps = [(c, b) for c in range(comps) for b in range(blocks)]
     copies = [
         pltpu.make_async_copy(snap.at[b, c], buf.at[b, c], sems.at[i])
         for i, (c, b) in enumerate(steps)
     ]
-    table_copy = pltpu.make_async_copy(table_hbm, table, small.at[0])
+    table_copy = pltpu.make_async_copy(table_hbm, thin, small.at[0])
     quad_copy = pltpu.make_async_copy(quad_hbm, quad, small.at[1])
     table_copy.start()
     quad_copy.start()
     for copy in copies[:IN_FLIGHT]:
         copy.start()
     me = lax.axis_index("blk")
+    height = piles.shape[1]
     table_copy.wait()
+    shape = (table.shape[0], thin.shape[0])
+    spread = jnp.where(iota(shape, 0) // blocks == iota(shape, 1), 1.0, 0.0).astype(BF16)
+    spread = jnp.dot(spread, thin[...], preferred_element_type=F32)
+    for b in range(blocks):
+        table[:, b * samples : (b + 1) * samples] = jnp.where(
+            iota(spread.shape, 0) % blocks == b, spread, 0.0
+        ).astype(BF16)
     quad_copy.wait()
     root = jnp.sqrt(quad[...])
-    height = piles.shape[1]
     for i, (c, b) in enumerate(steps):
         copies[i].wait()
         if i + IN_FLIGHT < len(copies):
@@ -195,35 +199,53 @@
 
 def packed_mm(left, right, full=True):
     high, middle, low = thirds(left)
+    top, mid, end = right
     group = iota(left.shape, 1) // WIDTH
-    first = jnp.where(group == 2, middle, high)
-    top, mid, end = right
-    total = jnp.dot(first, jnp.concatenate([top, mid, top, end], 0), preferred_element_type=F32)
+    terms = [top, mid, top, end]
+    lanes = jnp.where(group == 2, middle, high)
     if full:
-        second = jnp.where(group == 0, middle, low)[:, : 2 * WIDTH]
-        total = total + jnp.dot(second, jnp.concatenate([mid, top], 0), preferred_element_type=F32)
-    return total
-
-
-def inverse_roots(inners):
+        terms += [mid, top]
+        rest = jnp.where(group == 0, middle, low)[:, : 2 * WIDTH]
+        lanes = jnp.concatenate([lanes, rest], 1)
+    return jnp.dot(lanes, jnp.concatenate(terms, 0), preferred_element_type=F32)
+
+
+def inverse_roots(inners, lefts, rights):
     shape = inners[0].shape
     identity = jnp.where(iota(shape, 0) == iota(shape, 1) % WIDTH, 1.0, 0.0)
+    squares = [packed_mm(inner, thirds(inner)) for inner in inners]
     norms = [
         jnp.sqrt(jnp.sum(inner * inner, keepdims=True) * (1.0 / COPIES)) for inner in inners
     ]
-    rests = [identity - inner / norm for inner, norm in zip(inners, norms)]
-    roots = [identity + 0.5 * rest for rest in rests]
-    for step in range(1, NS_STEPS):
-        full = step <= FULL_STEPS
-        rights = [thirds(rest) for rest in rests]
-        squares = [packed_mm(e, r, full) for e, r in zip(rests, rights)]
-        cubes = [packed_mm(s, r, full) for s, r in zip(squares, rights)]
-        if step > 1:
-            roots = [z + 0.5 * packed_mm(z, r, full) for z, r in zip(roots, rights)]
+    scales = [1.0 / norm for norm in norms]
+    rests = [identity - inner * scale for inner, scale in zip(inners, scales)]
+    squares = [
+        2.0 * rest - identity + square * scale * scale
+        for rest, square, scale in zip(rests, squares, scales)
+    ]
+    roots = None
+    for step in range(NS_STEPS - 1):
+        full = step < FULL_STEPS
+        terms = [thirds(rest) for rest in rests]
+        if step > 0:
+            squares = [packed_mm(e, r, full) for e, r in zip(rests, terms)]
+            roots = [z + 0.5 * packed_mm(z, r, full) for z, r in zip(roots, terms)]
+        else:
+            roots = [identity + 0.5 * e for e in rests]
+        cubes = [packed_mm(s, r, full) for s, r in zip(squares, terms)]
         rests = [0.75 * s + 0.25 * c for s, c in zip(squares, cubes)]
-    rights = [thirds(rest) for rest in rests]
-    roots = [z + 0.5 * packed_mm(z, r, False) for z, r in zip(roots, rights)]
-    return [z * (1.0 / jnp.sqrt(norm)) for z, norm in zip(roots, norms)]
+    scales = [1.0 / jnp.sqrt(norm) for norm in norms]
+    lefts = [packed_mm(z, thirds(left)) for z, left in zip(roots, lefts)]
+    rights = [packed_mm(right, thirds(z)) for z, right in zip(roots, rights)]
+    lefts = [
+        (left + 0.5 * packed_mm(e, thirds(left), False)) * scale
+        for e, left, scale in zip(rests, lefts, scales)
+    ]
+    rights = [
+        (right + 0.5 * packed_mm(right, thirds(e), False)) * scale
+        for e, right, scale in zip(rests, rights, scales)
+    ]
+    return lefts, rights
 
 
 def subspace_kernel(share, blocks, dofs, grams, *refs):
@@ -235,32 +257,21 @@
     freqs = range(share)
     tall_next = mm(tall[...], gram)
     images = [mm(gram, mm(gram, wide[f])) for f in freqs]
-    for step in range(ITERS):
-        rows = [tall_next[f * WIDTH : (f + 1) * WIDTH] for f in freqs]
+    rows = [tall_next[f * WIDTH : (f + 1) * WIDTH] for f in freqs]
+    for _ in range(ITERS - 1):
         inners = [mm(rows[f], images[f]) for f in freqs]
-        if step < ITERS - 1:
-            tall_image = mm(tall_next, gram)
-            ahead = [mm(gram, image) for image in images]
-        roots = inverse_roots(inners)
-        rights = [thirds(root) for root in roots]
-        if step < ITERS - 1:
-            tall_next = jnp.concatenate(
-                [
-                    packed_mm(roots[f], thirds(tall_image[f * WIDTH : (f + 1) * WIDTH]))
-                    for f in freqs
-                ],
-                0,
-            )
-            images = [packed_mm(ahead[f], rights[f]) for f in freqs]
+        tall_image = mm(jnp.concatenate(rows, 0), gram)
+        ahead = [mm(gram, image) for image in images]
+        rows = [tall_image[f * WIDTH : (f + 1) * WIDTH] for f in freqs]
+        rows, images = inverse_roots(inners, rows, ahead)
+    inners = [mm(rows[f], images[f]) for f in freqs]
+    coefs, finals = inverse_roots(inners, rows, images)
     half = share * blocks
     me = lax.axis_index("blk")
     energy_out[...] = jnp.zeros_like(energy_out)
-    for f in freqs:
-        final = packed_mm(images[f], rights[f])
+    for f, (coef, final) in enumerate(zip(coefs, finals)):
         energy = jnp.sum(final * final, axis=0, keepdims=True)
         energy_out[pl.ds(me * share + f, 1), :] = energy[:, :RANK]
-    for f in freqs:
-        coef = packed_mm(roots[f], thirds(rows[f]))
         same = (iota(coef.shape, 0) // RANK + iota(coef.shape, 1) // half) % 2 == 0
         coef_out[f * WIDTH : (f + 1) * WIDTH] = jnp.where(same, coef, -coef).astype(BF16)
 
@@ -307,7 +318,7 @@
     size = groups * height
     piece = (height, width)
 
-    table = in_hbm(jnp.asarray(wide_table(samples, groups, blocks)))
+    table = in_hbm(jnp.asarray(table_rows(samples, groups)))
     quad = quadrature.reshape(1, points)
     steps = blocks * comps
     spectra = call(
@@ -319,6 +330,7 @@
             pltpu.VMEM((blocks, comps, samples, points), BF16),
             pltpu.VMEM(table.shape, BF16),
             pltpu.VMEM((1, points), F32),
+            pltpu.VMEM((size, blocks * samples), BF16),
             pltpu.VMEM((groups, *piece), BF16),
             pltpu.SemaphoreType.DMA((steps,)),
             pltpu.SemaphoreType.DMA((2,)),

time: 44.9 us -> 44.1 us (0.982)
  Pallas kernels: 15.8 us -> 15 us
    pallas_call x1, Pallas kernels: 8.97 us -> 8.27 us  [per_device(): call(functools.partial(subspace_kernel, share, blocks, width * spaces, le...]
where the time goes in v3:
time: 44.1 us; the launch traced here: 43.9 us
  Pallas kernels  15 us (34%)
  starting transfers between devices  13.8 us (31%)
  waiting for transfers between devices  13.8 us (31%)
  between operations  0.73 us (2%)
  other arithmetic  0.64 us (1%)
    ppermute x11, starting transfers between devices, exchange(): return lax.ppermute(array, axis, [(i, i ^ distance) for i in range(size)])  13.8 us
    ppermute x11, waiting for transfers between devices, exchange(): return lax.ppermute(array, axis, [(i, i ^ distance) for i in range(size)])  13.8 us
    pallas_call x1, Pallas kernels, per_device(): call(functools.partial(subspace_kernel, share, blocks, width * spaces, le...  8.27 us
    pallas_call x1, Pallas kernels, per_device(): call(functools.partial(spectra_kernel, groups), [jax.ShapeDtypeStruct((2,...  3.89 us
    pallas_call x1, Pallas kernels, per_device(): call(functools.partial(start_kernel, share, blocks), [jax.ShapeDtypeStruc...  1.53 us
    pallas_call x1, Pallas kernels, per_device(): call(functools.partial(modes_kernel, share), jax.ShapeDtypeStruct((share,...  0.95 us
  transfers between devices with their start and end apart: 11, of which 8 were waited for; matrix products, arithmetic and copies ran while one was open for 0% of the time, Pallas kernels for 6%

profile of v3, /device:TPU:0, one launch (start us, length us, event | category | flops | bytes accessed | tf_op | source)
XLA Modules:
  0.0 43.9 jit_solution(14388687998154719272)
XLA Ops:
  0.6 0.0 copy-start
  0.6 3.9 %spectra.1 = (bf16[2,16,1536]{2,1,0:T(8,128)(2,1)S(1)}, bf16[2,16,1536]{2,1,0:T(8,128)(2,1)S(1)}, bf16[2,16,1536]{2,1,0:T(8,128)(2,1)S(1)}, bf16[2,16,1536]{2,1,0:T(8,128)(2,1)S(1)}) custom-call(bf16[4,3,512,512]{3,2,1,0:T(8,128)(2,1)} %bitcast.22, bf16[32,512]{1,0:T(8,128)(2,1)} %constant.2.clone.table_hbm, f32[1,512]{1,0:T(1,128)} %bitcast.20), custom_call_target="tpu_custom_call" | custom-call | tf_op jit(solution)/shard_map/spectra/pallas_call | solution.py:324
  4.5 3.1 %collective-permute-start = (bf16[2,16,1536]{2,1,0:T(8,128)(2,1)S(1)}, bf16[2,16,1536]{2,1,0:T(8,128)(2,1)S(1)}, u32[]{:S(2)}, u32[]{:S(2)}) collective-permute-start(bf16[2,16,1536]{2,1,0:T(8,128)(2,1)S(1)} %get-tuple-element.18), channel_id=1, source_target_pairs={{0,2},{1,3},{2,0},{3,1},{4,6},{5,7},{6,4},{7,5},{8,10},{9,11},{10,... | collective-permute-start | bytes 294920 | tf_op jit(solution)/shard_map/ppermute | solution.py:308
  7.6 2.6 %collective-permute-start.1 = (bf16[2,16,1536]{2,1,0:T(8,128)(2,1)S(1)}, bf16[2,16,1536]{2,1,0:T(8,128)(2,1)S(1)}, u32[]{:S(2)}, u32[]{:S(2)}) collective-permute-start(bf16[2,16,1536]{2,1,0:T(8,128)(2,1)S(1)} %get-tuple-element.19), channel_id=1, source_target_pairs={{0,4},{1,5},{2,6},{3,7},{4,0},{5,1},{6,2},{7,3},{8,12},{9,13},{10,... | collective-permute-start | bytes 294920 | tf_op jit(solution)/shard_map/ppermute | solution.py:308
  10.2 0.0 collective-permute-start.2
  10.2 1.5 %start.1 = (f32[2,128,128]{2,1,0:T(8,128)S(1)}, f32[64,128]{1,0:T(8,128)S(1)}) custom-call(f32[16,2,16,32]{3,2,1,0:T(8,128)} %bitcast.24, bf16[2,16,1536]{2,1,0:T(8,128)(2,1)S(1)} %get-tuple-element.15._), custom_call_target="tpu_custom_call" | custom-call | tf_op jit(solution)/shard_map/start/pallas_call | solution.py:340
  11.8 0.0 collective-permute-done
  11.8 6.3 %collective-permute-done.1 = bf16[2,16,1536]{2,1,0:T(8,128)(2,1)S(1)} collective-permute-done((bf16[2,16,1536]{2,1,0:T(8,128)(2,1)S(1)}, bf16[2,16,1536]{2,1,0:T(8,128)(2,1)S(1)}, u32[]{:S(2)}, u32[]{:S(2)}) %collective-permute-start.1) | collective-permute-done | bytes 98336 | tf_op jit(solution)/shard_map/ppermute | solution.py:308
  18.0 0.0 collective-permute-done.2
  18.1 0.1 collective-permute-start.3
  18.2 1.4 %collective-permute-done.3 = bf16[4,16,1536]{2,1,0:T(8,128)(2,1)S(1)} collective-permute-done((bf16[4,16,1536]{2,1,0:T(8,128)(2,1)S(1)}, bf16[4,16,1536]{2,1,0:T(8,128)(2,1)S(1)}, u32[]{:S(2)}, u32[]{:S(2)}) %collective-permute-start.3) | collective-permute-done | bytes 196640 | tf_op jit(solution)/shard_map/ppermute | solution.py:308
  19.6 0.3 gram.1.refs_0_
  20.0 2.5 %collective-permute-start.6 = (f32[32,128]{1,0:T(8,128)S(1)}, f32[32,128]{1,0:T(8,128)S(1)}, u32[]{:S(2)}, u32[]{:S(2)}) collective-permute-start(f32[32,128]{1,0:T(8,128)S(1)} %gram.1.refs_0_), channel_id=1, source_target_pairs={{0,24},{8,16},{16,8},{24,0},{1,25},{9,17},{17,9},{25,1},{2,26},{10... | collective-permute-start | bytes 49160 | tf_op jit(solution)/shard_map/ppermute | solution.py:308
  22.5 0.5 %collective-permute-start.5 = (f32[32,128]{1,0:T(8,128)S(1)}, f32[32,128]{1,0:T(8,128)S(1)}, u32[]{:S(2)}, u32[]{:S(2)}) collective-permute-start(f32[32,128]{1,0:T(8,128)S(1)} %gram.1.refs_0_), channel_id=1, source_target_pairs={{0,16},{8,24},{16,0},{24,8},{1,17},{9,25},{17,1},{25,9},{2,18},{10... | collective-permute-start | bytes 49160 | tf_op jit(solution)/shard_map/ppermute | solution.py:308
  23.0 0.5 %collective-permute-start.4 = (f32[32,128]{1,0:T(8,128)S(1)}, f32[32,128]{1,0:T(8,128)S(1)}, u32[]{:S(2)}, u32[]{:S(2)}) collective-permute-start(f32[32,128]{1,0:T(8,128)S(1)} %gram.1.refs_0_), channel_id=1, source_target_pairs={{0,8},{8,0},{16,24},{24,16},{1,9},{9,1},{17,25},{25,17},{2,10},{10... | collective-permute-start | bytes 49160 | tf_op jit(solution)/shard_map/ppermute | solution.py:308
  23.5 1.1 %collective-permute-done.6.refs_3_ = f32[32,128]{1,0:T(8,128)S(1)} collective-permute-done((f32[32,128]{1,0:T(8,128)S(1)}, f32[32,128]{1,0:T(8,128)S(1)}, u32[]{:S(2)}, u32[]{:S(2)}) %collective-permute-start.6) | collective-permute-done | bytes 16416 | tf_op jit(solution)/shard_map/ppermute | solution.py:308
  24.7 1.6 %collective-permute-done.5.refs_2_ = f32[32,128]{1,0:T(8,128)S(1)} collective-permute-done((f32[32,128]{1,0:T(8,128)S(1)}, f32[32,128]{1,0:T(8,128)S(1)}, u32[]{:S(2)}, u32[]{:S(2)}) %collective-permute-start.5) | collective-permute-done | bytes 16416 | tf_op jit(solution)/shard_map/ppermute | solution.py:308
  26.3 0.5 %collective-permute-done.4.refs_1_ = f32[32,128]{1,0:T(8,128)S(1)} collective-permute-done((f32[32,128]{1,0:T(8,128)S(1)}, f32[32,128]{1,0:T(8,128)S(1)}, u32[]{:S(2)}, u32[]{:S(2)}) %collective-permute-start.4) | collective-permute-done | bytes 16416 | tf_op jit(solution)/shard_map/ppermute | solution.py:308
  26.7 8.3 %subspace.1 = (bf16[64,128]{1,0:T(8,128)(2,1)S(1)}, f32[16,16]{1,0:T(8,128)S(1)}) custom-call(f32[32,128]{1,0:T(8,128)S(1)} %gram.1.refs_0_, f32[32,128]{1,0:T(8,128)S(1)} %collective-permute-done.4.refs_1_, f32[32,128]{1,0:T(8,128)S(1)} %collective-permute-done.5.refs_2_, f32[32,128]{1,0:T(8,128)S(1)} %collective-permute-done.6.refs_3_, ...), custom_call_target="tpu_custom_call" | custom-call | tf_op jit(solution)/shard_map/subspace/pallas_call | solution.py:369
  35.0 0.1 collective-permute-start.7
  35.1 1.2 %collective-permute-done.7 = f32[16,16]{1,0:T(8,128)S(1)} collective-permute-done((f32[16,16]{1,0:T(8,128)S(1)}, f32[16,16]{1,0:T(8,128)S(1)}, u32[]{:S(2)}, u32[]{:S(2)}) %collective-permute-start.7) | collective-permute-done | bytes 1056 | tf_op jit(solution)/shard_map/ppermute | solution.py:308
  36.3 2.5 %collective-permute-start.10 = (f32[16,16]{1,0:T(8,128)S(1)}, f32[16,16]{1,0:T(8,128)S(1)}, u32[]{:S(2)}, u32[]{:S(2)}) collective-permute-start(f32[16,16]{1,0:T(8,128)S(1)} %add.12), channel_id=1, source_target_pairs={{0,6},{1,7},{2,4},{3,5},{4,2},{5,3},{6,0},{7,1},{8,14},{9,15},{10,... | collective-permute-start | bytes 3080 | tf_op jit(solution)/shard_map/ppermute | solution.py:308
  38.7 0.6 %collective-permute-start.9 = (f32[16,16]{1,0:T(8,128)S(1)}, f32[16,16]{1,0:T(8,128)S(1)}, u32[]{:S(2)}, u32[]{:S(2)}) collective-permute-start(f32[16,16]{1,0:T(8,128)S(1)} %add.12), channel_id=1, source_target_pairs={{0,4},{1,5},{2,6},{3,7},{4,0},{5,1},{6,2},{7,3},{8,12},{9,13},{10,... | collective-permute-start | bytes 3080 | tf_op jit(solution)/shard_map/ppermute | solution.py:308
  39.3 1.3 %collective-permute-start.8 = (f32[16,16]{1,0:T(8,128)S(1)}, f32[16,16]{1,0:T(8,128)S(1)}, u32[]{:S(2)}, u32[]{:S(2)}) collective-permute-start(f32[16,16]{1,0:T(8,128)S(1)} %add.12), channel_id=1, source_target_pairs={{0,2},{1,3},{2,0},{3,1},{4,6},{5,7},{6,4},{7,5},{8,10},{9,11},{10,... | collective-permute-start | bytes 3080 | tf_op jit(solution)/shard_map/ppermute | solution.py:308
  40.6 0.0 copy-done
  40.7 0.9 %modes.1 = f32[2,2,3,16,512]{4,3,2,1,0:T(8,128)} custom-call(f32[1,512]{1,0:T(1,128)S(1)} %bitcast.21, bf16[64,128]{1,0:T(8,128)(2,1)S(1)} %get-tuple-element.26.coef, bf16[16,1536]{1,0:T(8,128)(2,1)S(1)} %get-tuple-element.39.refs_0_, bf16[16,1536]{1,0:T(8,128)(2,1)S(1)} %get-tuple-element.31.refs_1_, bf16[16,1536]{1,0:T(8,128)(2,1)S(1)} %get-tuple-element.36.refs_2_, ...), custom_call_target="tpu_custom_call" | custom-call | tf_op jit(solution)/shard_map/modes/pallas_call | solution.py:379
  41.6 0.1 collective-permute-done.10
  41.7 1.6 %collective-permute-done.9 = f32[16,16]{1,0:T(8,128)S(1)} collective-permute-done((f32[16,16]{1,0:T(8,128)S(1)}, f32[16,16]{1,0:T(8,128)S(1)}, u32[]{:S(2)}, u32[]{:S(2)}) %collective-permute-start.9) | collective-permute-done | bytes 1056 | tf_op jit(solution)/shard_map/ppermute | solution.py:308
  43.3 0.0 collective-permute-done.8
  43.3 0.6 %add_add_fusion = f32[16,16]{1,0:T(8,128)} fusion(f32[16,16]{1,0:T(8,128)S(1)} %collective-permute-done.10, f32[16,16]{1,0:T(8,128)S(1)} %collective-permute-done.9, f32[16,16]{1,0:T(8,128)S(1)} %add.12, f32[16,16]{1,0:T(8,128)S(1)} %collective-permute-done.8), kind=kLoop, calls=%fused_computation.9 | loop fusion | flops 768 | bytes 5120 | tf_op jit(solution)/shard_map/add | solution.py:389
  (6 shorter events, 0.1 us)
Async XLA Ops:
  0.6 40.0 %copy-start = (f32[512]{0:T(512)S(1)}, f32[512]{0:T(512)}, u32[]{:S(2)}) copy-start(f32[512]{0:T(512)} %param.5) | copy-start | bytes 6148
  4.5 7.2 %collective-permute-start = (bf16[2,16,1536]{2,1,0:T(8,128)(2,1)S(1)}, bf16[2,16,1536]{2,1,0:T(8,128)(2,1)S(1)}, u32[]{:S(2)}, u32[]{:S(2)}) collective-permute-start(bf16[2,16,1536]{2,1,0:T(8,128)(2,1)S(1)} %get-tuple-element.18), channel_id=1, source_target_pairs={{0,2},{1,3},{2,0},{3,1},{4,6},{5,7},{6,4},{7,5},{8,10},{9,11},{10,... | collective-permute-start | bytes 294920 | tf_op jit(solution)/shard_map/ppermute | solution.py:308
  7.6 10.4 %collective-permute-start.1 = (bf16[2,16,1536]{2,1,0:T(8,128)(2,1)S(1)}, bf16[2,16,1536]{2,1,0:T(8,128)(2,1)S(1)}, u32[]{:S(2)}, u32[]{:S(2)}) collective-permute-start(bf16[2,16,1536]{2,1,0:T(8,128)(2,1)S(1)} %get-tuple-element.19), channel_id=1, source_target_pairs={{0,4},{1,5},{2,6},{3,7},{4,0},{5,1},{6,2},{7,3},{8,12},{9,13},{10,... | collective-permute-start | bytes 294920 | tf_op jit(solution)/shard_map/ppermute | solution.py:308
  10.2 7.8 %collective-permute-start.2 = (bf16[2,16,1536]{2,1,0:T(8,128)(2,1)S(1)}, bf16[2,16,1536]{2,1,0:T(8,128)(2,1)S(1)}, u32[]{:S(2)}, u32[]{:S(2)}) collective-permute-start(bf16[2,16,1536]{2,1,0:T(8,128)(2,1)S(1)} %get-tuple-element.20), channel_id=1, source_target_pairs={{0,6},{1,7},{2,4},{3,5},{4,2},{5,3},{6,0},{7,1},{8,14},{9,15},{10,... | collective-permute-start | bytes 294920 | tf_op jit(solution)/shard_map/ppermute | solution.py:308
  18.1 1.5 %collective-permute-start.3 = (bf16[4,16,1536]{2,1,0:T(8,128)(2,1)S(1)}, bf16[4,16,1536]{2,1,0:T(8,128)(2,1)S(1)}, u32[]{:S(2)}, u32[]{:S(2)}) collective-permute-start(bf16[4,16,1536]{2,1,0:T(8,128)(2,1)S(1)} %pad_maximum_fusion), channel_id=1, source_target_pairs={{0,1},{1,0},{2,3},{3,2},{4,5},{5,4},{6,7},{7,6},{8,9},{9,8},{10,11... | collective-permute-start | bytes 589832 | tf_op jit(solution)/shard_map/ppermute | solution.py:308
  20.0 4.7 %collective-permute-start.6 = (f32[32,128]{1,0:T(8,128)S(1)}, f32[32,128]{1,0:T(8,128)S(1)}, u32[]{:S(2)}, u32[]{:S(2)}) collective-permute-start(f32[32,128]{1,0:T(8,128)S(1)} %gram.1.refs_0_), channel_id=1, source_target_pairs={{0,24},{8,16},{16,8},{24,0},{1,25},{9,17},{17,9},{25,1},{2,26},{10... | collective-permute-start | bytes 49160 | tf_op jit(solution)/shard_map/ppermute | solution.py:308
  22.5 3.7 %collective-permute-start.5 = (f32[32,128]{1,0:T(8,128)S(1)}, f32[32,128]{1,0:T(8,128)S(1)}, u32[]{:S(2)}, u32[]{:S(2)}) collective-permute-start(f32[32,128]{1,0:T(8,128)S(1)} %gram.1.refs_0_), channel_id=1, source_target_pairs={{0,16},{8,24},{16,0},{24,8},{1,17},{9,25},{17,1},{25,9},{2,18},{10... | collective-permute-start | bytes 49160 | tf_op jit(solution)/shard_map/ppermute | solution.py:308
  23.0 3.7 %collective-permute-start.4 = (f32[32,128]{1,0:T(8,128)S(1)}, f32[32,128]{1,0:T(8,128)S(1)}, u32[]{:S(2)}, u32[]{:S(2)}) collective-permute-start(f32[32,128]{1,0:T(8,128)S(1)} %gram.1.refs_0_), channel_id=1, source_target_pairs={{0,8},{8,0},{16,24},{24,16},{1,9},{9,1},{17,25},{25,17},{2,10},{10... | collective-permute-start | bytes 49160 | tf_op jit(solution)/shard_map/ppermute | solution.py:308
  35.0 1.2 %collective-permute-start.7 = (f32[16,16]{1,0:T(8,128)S(1)}, f32[16,16]{1,0:T(8,128)S(1)}, u32[]{:S(2)}, u32[]{:S(2)}) collective-permute-start(f32[16,16]{1,0:T(8,128)S(1)} %get-tuple-element.27), channel_id=1, source_target_pairs={{0,1},{1,0},{2,3},{3,2},{4,5},{5,4},{6,7},{7,6},{8,9},{9,8},{10,11... | collective-permute-start | bytes 3080 | tf_op jit(solution)/shard_map/ppermute | solution.py:308
  36.3 5.5 %collective-permute-start.10 = (f32[16,16]{1,0:T(8,128)S(1)}, f32[16,16]{1,0:T(8,128)S(1)}, u32[]{:S(2)}, u32[]{:S(2)}) collective-permute-start(f32[16,16]{1,0:T(8,128)S(1)} %add.12), channel_id=1, source_target_pairs={{0,6},{1,7},{2,4},{3,5},{4,2},{5,3},{6,0},{7,1},{8,14},{9,15},{10,... | collective-permute-start | bytes 3080 | tf_op jit(solution)/shard_map/ppermute | solution.py:308
  38.7 4.5 %collective-permute-start.9 = (f32[16,16]{1,0:T(8,128)S(1)}, f32[16,16]{1,0:T(8,128)S(1)}, u32[]{:S(2)}, u32[]{:S(2)}) collective-permute-start(f32[16,16]{1,0:T(8,128)S(1)} %add.12), channel_id=1, source_target_pairs={{0,4},{1,5},{2,6},{3,7},{4,0},{5,1},{6,2},{7,3},{8,12},{9,13},{10,... | collective-permute-start | bytes 3080 | tf_op jit(solution)/shard_map/ppermute | solution.py:308
  39.3 4.0 %collective-permute-start.8 = (f32[16,16]{1,0:T(8,128)S(1)}, f32[16,16]{1,0:T(8,128)S(1)}, u32[]{:S(2)}, u32[]{:S(2)}) collective-permute-start(f32[16,16]{1,0:T(8,128)S(1)} %add.12), channel_id=1, source_target_pairs={{0,2},{1,3},{2,0},{3,1},{4,6},{5,7},{6,4},{7,5},{8,10},{9,11},{10,... | collective-permute-start | bytes 3080 | tf_op jit(solution)/shard_map/ppermute | solution.py:308

commit v4 on v3

--- a/solution.py
+++ b/solution.py
@@ -348,11 +348,14 @@
         [pltpu.VMEM((share, 2, RANK, groups * blocks), F32), pltpu.SemaphoreType.DMA],
     )(in_hbm(omega.transpose(0, 1, 3, 2)), spectra[0])
 
-    arrived = {far: exchange(spectra[far], "blk", 2 * far) for far in range(reach - 1, 0, -1)}
-    wide, tall, arrived = lax.optimization_barrier((wide, tall, arrived))
+    arrived = {far: exchange(spectra[far], "blk", 2 * far) for far in range(1, reach)}
+    wide, tall, arrived[1] = lax.optimization_barrier((wide, tall, arrived[1]))
     arrived[0] = spectra[0]
-    sent = exchange(jnp.stack([arrived[far][1] for far in range(reach)]), "blk", 1)
-    pieces = [piece for far in range(reach) for piece in (arrived[far][0], sent[far])]
+    others = {}
+    for part in (range(1, reach, 2), range(0, reach, 2)):
+        sent = exchange(jnp.stack([arrived[far][1] for far in part]), "blk", 1)
+        others |= {far: sent[i] for i, far in enumerate(part)}
+    pieces = [piece for far in range(reach) for piece in (arrived[far][0], others[far])]
 
     packed = (size * (blocks if share * blocks == 8 else height) // height, size)
     gram = call(

time: 44.1 us -> 43 us (0.975)
  waiting for transfers between devices: 13.8 us -> 12.5 us
    ppermute x11 -> x12, waiting for transfers between devices: 13.8 us -> 12.5 us  [exchange(): return lax.ppermute(array, axis, [(i, i ^ distance) for i in range(size)])]
    ppermute x11 -> x12, starting transfers between devices: 13.8 us -> 13.8 us  [exchange(): return lax.ppermute(array, axis, [(i, i ^ distance) for i in range(size)])]
  transfers between devices with their start and end apart: 11 -> 12, of which waited for: 8 -> 9; matrix products, arithmetic and copies ran while one was open for 0% -> 0% of each run, Pallas kernels for 6% -> 6%
where the time goes in v4:
time: 43 us; the launch traced here: 42.8 us
  Pallas kernels  15 us (35%)
  starting transfers between devices  13.8 us (32%)
  waiting for transfers between devices  12.5 us (29%)
  between operations  0.76 us (2%)
  other arithmetic  0.63 us (1%)
    ppermute x12, starting transfers between devices, exchange(): return lax.ppermute(array, axis, [(i, i ^ distance) for i in range(size)])  13.8 us
    ppermute x12, waiting for transfers between devices, exchange(): return lax.ppermute(array, axis, [(i, i ^ distance) for i in range(size)])  12.5 us
    pallas_call x1, Pallas kernels, per_device(): call(functools.partial(subspace_kernel, share, blocks, width * spaces, le...  8.27 us
    pallas_call x1, Pallas kernels, per_device(): call(functools.partial(spectra_kernel, groups), [jax.ShapeDtypeStruct((2,...  3.89 us
    pallas_call x1, Pallas kernels, per_device(): call(functools.partial(start_kernel, share, blocks), [jax.ShapeDtypeStruc...  1.53 us
    pallas_call x1, Pallas kernels, per_device(): call(functools.partial(modes_kernel, share), jax.ShapeDtypeStruct((share,...  0.95 us
  transfers between devices with their start and end apart: 12, of which 9 were waited for; matrix products, arithmetic and copies ran while one was open for 0% of the time, Pallas kernels for 6%

profile of v4, /device:TPU:0, one launch (start us, length us, event | category | flops | bytes accessed | tf_op | source)
XLA Modules:
  0.0 42.8 jit_solution(16008151515859002545)
XLA Ops:
  0.6 0.0 copy-start
  0.6 3.9 %spectra.1 = (bf16[2,16,1536]{2,1,0:T(8,128)(2,1)S(1)}, bf16[2,16,1536]{2,1,0:T(8,128)(2,1)S(1)}, bf16[2,16,1536]{2,1,0:T(8,128)(2,1)S(1)}, bf16[2,16,1536]{2,1,0:T(8,128)(2,1)S(1)}) custom-call(bf16[4,3,512,512]{3,2,1,0:T(8,128)(2,1)} %bitcast.22, bf16[32,512]{1,0:T(8,128)(2,1)} %constant.2.clone.table_hbm, f32[1,512]{1,0:T(1,128)} %bitcast.20), custom_call_target="tpu_custom_call" | custom-call | tf_op jit(solution)/shard_map/spectra/pallas_call | solution.py:324
  4.5 4.1 %collective-permute-start = (bf16[2,16,1536]{2,1,0:T(8,128)(2,1)S(1)}, bf16[2,16,1536]{2,1,0:T(8,128)(2,1)S(1)}, u32[]{:S(2)}, u32[]{:S(2)}) collective-permute-start(bf16[2,16,1536]{2,1,0:T(8,128)(2,1)S(1)} %get-tuple-element.14), channel_id=1, source_target_pairs={{0,4},{1,5},{2,6},{3,7},{4,0},{5,1},{6,2},{7,3},{8,12},{9,13},{10,... | collective-permute-start | bytes 294920 | tf_op jit(solution)/shard_map/ppermute | solution.py:308
  8.6 1.6 %collective-permute-start.2 = (bf16[2,16,1536]{2,1,0:T(8,128)(2,1)S(1)}, bf16[2,16,1536]{2,1,0:T(8,128)(2,1)S(1)}, u32[]{:S(2)}, u32[]{:S(2)}) collective-permute-start(bf16[2,16,1536]{2,1,0:T(8,128)(2,1)S(1)} %get-tuple-element.17), channel_id=1, source_target_pairs={{0,2},{1,3},{2,0},{3,1},{4,6},{5,7},{6,4},{7,5},{8,10},{9,11},{10,... | collective-permute-start | bytes 294920 | tf_op jit(solution)/shard_map/ppermute | solution.py:308
  10.2 0.0 collective-permute-start.3
  10.2 1.5 %start.1 = (f32[2,128,128]{2,1,0:T(8,128)S(1)}, f32[64,128]{1,0:T(8,128)S(1)}) custom-call(f32[16,2,16,32]{3,2,1,0:T(8,128)} %bitcast.24, bf16[2,16,1536]{2,1,0:T(8,128)(2,1)S(1)} %get-tuple-element.13._), custom_call_target="tpu_custom_call" | custom-call | tf_op jit(solution)/shard_map/start/pallas_call | solution.py:340
  11.8 2.8 %collective-permute-done = bf16[2,16,1536]{2,1,0:T(8,128)(2,1)S(1)} collective-permute-done((bf16[2,16,1536]{2,1,0:T(8,128)(2,1)S(1)}, bf16[2,16,1536]{2,1,0:T(8,128)(2,1)S(1)}, u32[]{:S(2)}, u32[]{:S(2)}) %collective-permute-start) | collective-permute-done | bytes 98336 | tf_op jit(solution)/shard_map/ppermute | solution.py:308
  14.6 0.1 collective-permute-start.1
  14.7 0.0 collective-permute-done.2
  14.7 2.1 %collective-permute-done.3 = bf16[2,16,1536]{2,1,0:T(8,128)(2,1)S(1)} collective-permute-done((bf16[2,16,1536]{2,1,0:T(8,128)(2,1)S(1)}, bf16[2,16,1536]{2,1,0:T(8,128)(2,1)S(1)}, u32[]{:S(2)}, u32[]{:S(2)}) %collective-permute-start.3) | collective-permute-done | bytes 98336 | tf_op jit(solution)/shard_map/ppermute | solution.py:308
  16.8 0.1 collective-permute-start.4
  16.9 0.0 collective-permute-done.1
  16.9 1.3 %collective-permute-done.4 = bf16[2,16,1536]{2,1,0:T(8,128)(2,1)S(1)} collective-permute-done((bf16[2,16,1536]{2,1,0:T(8,128)(2,1)S(1)}, bf16[2,16,1536]{2,1,0:T(8,128)(2,1)S(1)}, u32[]{:S(2)}, u32[]{:S(2)}) %collective-permute-start.4) | collective-permute-done | bytes 98336 | tf_op jit(solution)/shard_map/ppermute | solution.py:308
  18.2 0.3 gram.1.refs_0_
  18.6 2.5 %collective-permute-start.7 = (f32[32,128]{1,0:T(8,128)S(1)}, f32[32,128]{1,0:T(8,128)S(1)}, u32[]{:S(2)}, u32[]{:S(2)}) collective-permute-start(f32[32,128]{1,0:T(8,128)S(1)} %gram.1.refs_0_), channel_id=1, source_target_pairs={{0,24},{8,16},{16,8},{24,0},{1,25},{9,17},{17,9},{25,1},{2,26},{10... | collective-permute-start | bytes 49160 | tf_op jit(solution)/shard_map/ppermute | solution.py:308
  21.0 0.5 %collective-permute-start.6 = (f32[32,128]{1,0:T(8,128)S(1)}, f32[32,128]{1,0:T(8,128)S(1)}, u32[]{:S(2)}, u32[]{:S(2)}) collective-permute-start(f32[32,128]{1,0:T(8,128)S(1)} %gram.1.refs_0_), channel_id=1, source_target_pairs={{0,16},{8,24},{16,0},{24,8},{1,17},{9,25},{17,1},{25,9},{2,18},{10... | collective-permute-start | bytes 49160 | tf_op jit(solution)/shard_map/ppermute | solution.py:308
  21.5 0.6 %collective-permute-start.5 = (f32[32,128]{1,0:T(8,128)S(1)}, f32[32,128]{1,0:T(8,128)S(1)}, u32[]{:S(2)}, u32[]{:S(2)}) collective-permute-start(f32[32,128]{1,0:T(8,128)S(1)} %gram.1.refs_0_), channel_id=1, source_target_pairs={{0,8},{8,0},{16,24},{24,16},{1,9},{9,1},{17,25},{25,17},{2,10},{10... | collective-permute-start | bytes 49160 | tf_op jit(solution)/shard_map/ppermute | solution.py:308
  22.1 1.1 %collective-permute-done.7.refs_3_ = f32[32,128]{1,0:T(8,128)S(1)} collective-permute-done((f32[32,128]{1,0:T(8,128)S(1)}, f32[32,128]{1,0:T(8,128)S(1)}, u32[]{:S(2)}, u32[]{:S(2)}) %collective-permute-start.7) | collective-permute-done | bytes 16416 | tf_op jit(solution)/shard_map/ppermute | solution.py:308
  23.3 1.5 %collective-permute-done.6.refs_2_ = f32[32,128]{1,0:T(8,128)S(1)} collective-permute-done((f32[32,128]{1,0:T(8,128)S(1)}, f32[32,128]{1,0:T(8,128)S(1)}, u32[]{:S(2)}, u32[]{:S(2)}) %collective-permute-start.6) | collective-permute-done | bytes 16416 | tf_op jit(solution)/shard_map/ppermute | solution.py:308
  24.8 0.5 %collective-permute-done.5.refs_1_ = f32[32,128]{1,0:T(8,128)S(1)} collective-permute-done((f32[32,128]{1,0:T(8,128)S(1)}, f32[32,128]{1,0:T(8,128)S(1)}, u32[]{:S(2)}, u32[]{:S(2)}) %collective-permute-start.5) | collective-permute-done | bytes 16416 | tf_op jit(solution)/shard_map/ppermute | solution.py:308
  25.3 8.3 %subspace.1 = (bf16[64,128]{1,0:T(8,128)(2,1)S(1)}, f32[16,16]{1,0:T(8,128)S(1)}) custom-call(f32[32,128]{1,0:T(8,128)S(1)} %gram.1.refs_0_, f32[32,128]{1,0:T(8,128)S(1)} %collective-permute-done.5.refs_1_, f32[32,128]{1,0:T(8,128)S(1)} %collective-permute-done.6.refs_2_, f32[32,128]{1,0:T(8,128)S(1)} %collective-permute-done.7.refs_3_, ...), custom_call_target="tpu_custom_call" | custom-call | tf_op jit(solution)/shard_map/subspace/pallas_call | solution.py:372
  33.6 0.1 collective-permute-start.8
  33.6 1.2 %collective-permute-done.8 = f32[16,16]{1,0:T(8,128)S(1)} collective-permute-done((f32[16,16]{1,0:T(8,128)S(1)}, f32[16,16]{1,0:T(8,128)S(1)}, u32[]{:S(2)}, u32[]{:S(2)}) %collective-permute-start.8) | collective-permute-done | bytes 1056 | tf_op jit(solution)/shard_map/ppermute | solution.py:308
  34.8 2.8 %collective-permute-start.11 = (f32[16,16]{1,0:T(8,128)S(1)}, f32[16,16]{1,0:T(8,128)S(1)}, u32[]{:S(2)}, u32[]{:S(2)}) collective-permute-start(f32[16,16]{1,0:T(8,128)S(1)} %add.12), channel_id=1, source_target_pairs={{0,6},{1,7},{2,4},{3,5},{4,2},{5,3},{6,0},{7,1},{8,14},{9,15},{10,... | collective-permute-start | bytes 3080 | tf_op jit(solution)/shard_map/ppermute | solution.py:308
  37.6 0.8 %collective-permute-start.10 = (f32[16,16]{1,0:T(8,128)S(1)}, f32[16,16]{1,0:T(8,128)S(1)}, u32[]{:S(2)}, u32[]{:S(2)}) collective-permute-start(f32[16,16]{1,0:T(8,128)S(1)} %add.12), channel_id=1, source_target_pairs={{0,4},{1,5},{2,6},{3,7},{4,0},{5,1},{6,2},{7,3},{8,12},{9,13},{10,... | collective-permute-start | bytes 3080 | tf_op jit(solution)/shard_map/ppermute | solution.py:308
  38.4 0.8 %collective-permute-start.9 = (f32[16,16]{1,0:T(8,128)S(1)}, f32[16,16]{1,0:T(8,128)S(1)}, u32[]{:S(2)}, u32[]{:S(2)}) collective-permute-start(f32[16,16]{1,0:T(8,128)S(1)} %add.12), channel_id=1, source_target_pairs={{0,2},{1,3},{2,0},{3,1},{4,6},{5,7},{6,4},{7,5},{8,10},{9,11},{10,... | collective-permute-start | bytes 3080 | tf_op jit(solution)/shard_map/ppermute | solution.py:308
  39.2 0.0 copy-done
  39.2 0.9 %modes.1 = f32[2,2,3,16,512]{4,3,2,1,0:T(8,128)} custom-call(f32[1,512]{1,0:T(1,128)S(1)} %bitcast.21, bf16[64,128]{1,0:T(8,128)(2,1)S(1)} %get-tuple-element.22.coef, bf16[16,1536]{1,0:T(8,128)(2,1)S(1)} %get-tuple-element.35.refs_0_, bf16[16,1536]{1,0:T(8,128)(2,1)S(1)} %get-tuple-element.29.refs_1_, bf16[16,1536]{1,0:T(8,128)(2,1)S(1)} %get-tuple-element.33.refs_2_, ...), custom_call_target="tpu_custom_call" | custom-call | tf_op jit(solution)/shard_map/modes/pallas_call | solution.py:382
  40.1 0.1 collective-permute-done.11
  40.2 1.9 %collective-permute-done.10 = f32[16,16]{1,0:T(8,128)S(1)} collective-permute-done((f32[16,16]{1,0:T(8,128)S(1)}, f32[16,16]{1,0:T(8,128)S(1)}, u32[]{:S(2)}, u32[]{:S(2)}) %collective-permute-start.10) | collective-permute-done | bytes 1056 | tf_op jit(solution)/shard_map/ppermute | solution.py:308
  42.2 0.0 collective-permute-done.9
  42.2 0.6 %add_add_fusion = f32[16,16]{1,0:T(8,128)} fusion(f32[16,16]{1,0:T(8,128)S(1)} %collective-permute-done.11, f32[16,16]{1,0:T(8,128)S(1)} %collective-permute-done.10, f32[16,16]{1,0:T(8,128)S(1)} %add.12, f32[16,16]{1,0:T(8,128)S(1)} %collective-permute-done.9), kind=kLoop, calls=%fused_computation.10 | loop fusion | flops 768 | bytes 5120 | tf_op jit(solution)/shard_map/add | solution.py:392
  (9 shorter events, 0.1 us)
Async XLA Ops:
  0.6 38.6 %copy-start = (f32[512]{0:T(512)S(1)}, f32[512]{0:T(512)}, u32[]{:S(2)}) copy-start(f32[512]{0:T(512)} %param.5) | copy-start | bytes 6148
  4.5 10.0 %collective-permute-start = (bf16[2,16,1536]{2,1,0:T(8,128)(2,1)S(1)}, bf16[2,16,1536]{2,1,0:T(8,128)(2,1)S(1)}, u32[]{:S(2)}, u32[]{:S(2)}) collective-permute-start(bf16[2,16,1536]{2,1,0:T(8,128)(2,1)S(1)} %get-tuple-element.14), channel_id=1, source_target_pairs={{0,4},{1,5},{2,6},{3,7},{4,0},{5,1},{6,2},{7,3},{8,12},{9,13},{10,... | collective-permute-start | bytes 294920 | tf_op jit(solution)/shard_map/ppermute | solution.py:308
  8.6 6.1 %collective-permute-start.2 = (bf16[2,16,1536]{2,1,0:T(8,128)(2,1)S(1)}, bf16[2,16,1536]{2,1,0:T(8,128)(2,1)S(1)}, u32[]{:S(2)}, u32[]{:S(2)}) collective-permute-start(bf16[2,16,1536]{2,1,0:T(8,128)(2,1)S(1)} %get-tuple-element.17), channel_id=1, source_target_pairs={{0,2},{1,3},{2,0},{3,1},{4,6},{5,7},{6,4},{7,5},{8,10},{9,11},{10,... | collective-permute-start | bytes 294920 | tf_op jit(solution)/shard_map/ppermute | solution.py:308
  10.2 6.6 %collective-permute-start.3 = (bf16[2,16,1536]{2,1,0:T(8,128)(2,1)S(1)}, bf16[2,16,1536]{2,1,0:T(8,128)(2,1)S(1)}, u32[]{:S(2)}, u32[]{:S(2)}) collective-permute-start(bf16[2,16,1536]{2,1,0:T(8,128)(2,1)S(1)} %get-tuple-element.19), channel_id=1, source_target_pairs={{0,6},{1,7},{2,4},{3,5},{4,2},{5,3},{6,0},{7,1},{8,14},{9,15},{10,... | collective-permute-start | bytes 294920 | tf_op jit(solution)/shard_map/ppermute | solution.py:308
  14.6 2.3 %collective-permute-start.1 = (bf16[2,16,1536]{2,1,0:T(8,128)(2,1)S(1)}, bf16[2,16,1536]{2,1,0:T(8,128)(2,1)S(1)}, u32[]{:S(2)}, u32[]{:S(2)}) collective-permute-start(bf16[2,16,1536]{2,1,0:T(8,128)(2,1)S(1)} %pad_maximum_fusion), channel_id=1, source_target_pairs={{0,1},{1,0},{2,3},{3,2},{4,5},{5,4},{6,7},{7,6},{8,9},{9,8},{10,11... | collective-permute-start | bytes 294920 | tf_op jit(solution)/shard_map/ppermute | solution.py:308
  16.8 1.4 %collective-permute-start.4 = (bf16[2,16,1536]{2,1,0:T(8,128)(2,1)S(1)}, bf16[2,16,1536]{2,1,0:T(8,128)(2,1)S(1)}, u32[]{:S(2)}, u32[]{:S(2)}) collective-permute-start(bf16[2,16,1536]{2,1,0:T(8,128)(2,1)S(1)} %pad_maximum_fusion.1), channel_id=1, source_target_pairs={{0,1},{1,0},{2,3},{3,2},{4,5},{5,4},{6,7},{7,6},{8,9},{9,8},{10,11... | collective-permute-start | bytes 294920 | tf_op jit(solution)/shard_map/ppermute | solution.py:308
  18.6 4.7 %collective-permute-start.7 = (f32[32,128]{1,0:T(8,128)S(1)}, f32[32,128]{1,0:T(8,128)S(1)}, u32[]{:S(2)}, u32[]{:S(2)}) collective-permute-start(f32[32,128]{1,0:T(8,128)S(1)} %gram.1.refs_0_), channel_id=1, source_target_pairs={{0,24},{8,16},{16,8},{24,0},{1,25},{9,17},{17,9},{25,1},{2,26},{10... | collective-permute-start | bytes 49160 | tf_op jit(solution)/shard_map/ppermute | solution.py:308
  21.0 3.7 %collective-permute-start.6 = (f32[32,128]{1,0:T(8,128)S(1)}, f32[32,128]{1,0:T(8,128)S(1)}, u32[]{:S(2)}, u32[]{:S(2)}) collective-permute-start(f32[32,128]{1,0:T(8,128)S(1)} %gram.1.refs_0_), channel_id=1, source_target_pairs={{0,16},{8,24},{16,0},{24,8},{1,17},{9,25},{17,1},{25,9},{2,18},{10... | collective-permute-start | bytes 49160 | tf_op jit(solution)/shard_map/ppermute | solution.py:308
  21.5 3.7 %collective-permute-start.5 = (f32[32,128]{1,0:T(8,128)S(1)}, f32[32,128]{1,0:T(8,128)S(1)}, u32[]{:S(2)}, u32[]{:S(2)}) collective-permute-start(f32[32,128]{1,0:T(8,128)S(1)} %gram.1.refs_0_), channel_id=1, source_target_pairs={{0,8},{8,0},{16,24},{24,16},{1,9},{9,1},{17,25},{25,17},{2,10},{10... | collective-permute-start | bytes 49160 | tf_op jit(solution)/shard_map/ppermute | solution.py:308
  33.6 1.2 %collective-permute-start.8 = (f32[16,16]{1,0:T(8,128)S(1)}, f32[16,16]{1,0:T(8,128)S(1)}, u32[]{:S(2)}, u32[]{:S(2)}) collective-permute-start(f32[16,16]{1,0:T(8,128)S(1)} %get-tuple-element.23), channel_id=1, source_target_pairs={{0,1},{1,0},{2,3},{3,2},{4,5},{5,4},{6,7},{7,6},{8,9},{9,8},{10,11... | collective-permute-start | bytes 3080 | tf_op jit(solution)/shard_map/ppermute | solution.py:308
  34.8 5.4 %collective-permute-start.11 = (f32[16,16]{1,0:T(8,128)S(1)}, f32[16,16]{1,0:T(8,128)S(1)}, u32[]{:S(2)}, u32[]{:S(2)}) collective-permute-start(f32[16,16]{1,0:T(8,128)S(1)} %add.12), channel_id=1, source_target_pairs={{0,6},{1,7},{2,4},{3,5},{4,2},{5,3},{6,0},{7,1},{8,14},{9,15},{10,... | collective-permute-start | bytes 3080 | tf_op jit(solution)/shard_map/ppermute | solution.py:308
  37.6 4.6 %collective-permute-start.10 = (f32[16,16]{1,0:T(8,128)S(1)}, f32[16,16]{1,0:T(8,128)S(1)}, u32[]{:S(2)}, u32[]{:S(2)}) collective-permute-start(f32[16,16]{1,0:T(8,128)S(1)} %add.12), channel_id=1, source_target_pairs={{0,4},{1,5},{2,6},{3,7},{4,0},{5,1},{6,2},{7,3},{8,12},{9,13},{10,... | collective-permute-start | bytes 3080 | tf_op jit(solution)/shard_map/ppermute | solution.py:308
  38.4 3.7 %collective-permute-start.9 = (f32[16,16]{1,0:T(8,128)S(1)}, f32[16,16]{1,0:T(8,128)S(1)}, u32[]{:S(2)}, u32[]{:S(2)}) collective-permute-start(f32[16,16]{1,0:T(8,128)S(1)} %add.12), channel_id=1, source_target_pairs={{0,2},{1,3},{2,0},{3,1},{4,6},{5,7},{6,4},{7,5},{8,10},{9,11},{10,... | collective-permute-start | bytes 3080 | tf_op jit(solution)/shard_map/ppermute | solution.py:308

commit v5 on v4

--- a/solution.py
+++ b/solution.py
@@ -69,8 +69,8 @@
     quad_copy = pltpu.make_async_copy(quad_hbm, quad, small.at[1])
     table_copy.start()
     quad_copy.start()
-    for copy in copies[:IN_FLIGHT]:
-        copy.start()
+    for i, copy in enumerate(copies[:IN_FLIGHT]):
+        copy.start(priority=int(i < blocks))
     me = lax.axis_index("blk")
     height = piles.shape[1]
     table_copy.wait()

time: 43 us -> 42.7 us (level)
  transfers between devices with their start and end apart: 12 -> 12, of which waited for: 9 -> 10; matrix products, arithmetic and copies ran while one was open for 0% -> 0% of each run, Pallas kernels for 6% -> 6%
where the time goes in v5:
time: 42.7 us; the launch traced here: 42.5 us
  Pallas kernels  14.8 us (35%)
  starting transfers between devices  13.8 us (32%)
  waiting for transfers between devices  12.4 us (29%)
  between operations  0.76 us (2%)
  other arithmetic  0.63 us (1%)
    ppermute x12, starting transfers between devices, exchange(): return lax.ppermute(array, axis, [(i, i ^ distance) for i in range(size)])  13.8 us
    ppermute x12, waiting for transfers between devices, exchange(): return lax.ppermute(array, axis, [(i, i ^ distance) for i in range(size)])  12.4 us
    pallas_call x1, Pallas kernels, per_device(): call(functools.partial(subspace_kernel, share, blocks, width * spaces, le...  8.27 us
    pallas_call x1, Pallas kernels, per_device(): call(functools.partial(spectra_kernel, groups), [jax.ShapeDtypeStruct((2,...  3.74 us
    pallas_call x1, Pallas kernels, per_device(): call(functools.partial(start_kernel, share, blocks), [jax.ShapeDtypeStruc...  1.54 us
    pallas_call x1, Pallas kernels, per_device(): call(functools.partial(modes_kernel, share), jax.ShapeDtypeStruct((share,...  0.95 us
  transfers between devices with their start and end apart: 12, of which 10 were waited for; matrix products, arithmetic and copies ran while one was open for 0% of the time, Pallas kernels for 6%

profile of v5, /device:TPU:0, one launch (start us, length us, event | category | flops | bytes accessed | tf_op | source)
XLA Modules:
  0.0 42.5 jit_solution(17001885570673543940)
XLA Ops:
  0.6 0.0 copy-start
  0.6 3.7 %spectra.1 = (bf16[2,16,1536]{2,1,0:T(8,128)(2,1)S(1)}, bf16[2,16,1536]{2,1,0:T(8,128)(2,1)S(1)}, bf16[2,16,1536]{2,1,0:T(8,128)(2,1)S(1)}, bf16[2,16,1536]{2,1,0:T(8,128)(2,1)S(1)}) custom-call(bf16[4,3,512,512]{3,2,1,0:T(8,128)(2,1)} %bitcast.22, bf16[32,512]{1,0:T(8,128)(2,1)} %constant.2.clone.table_hbm, f32[1,512]{1,0:T(1,128)} %bitcast.20), custom_call_target="tpu_custom_call" | custom-call | tf_op jit(solution)/shard_map/spectra/pallas_call | solution.py:324
  4.4 4.1 %collective-permute-start = (bf16[2,16,1536]{2,1,0:T(8,128)(2,1)S(1)}, bf16[2,16,1536]{2,1,0:T(8,128)(2,1)S(1)}, u32[]{:S(2)}, u32[]{:S(2)}) collective-permute-start(bf16[2,16,1536]{2,1,0:T(8,128)(2,1)S(1)} %get-tuple-element.14), channel_id=1, source_target_pairs={{0,4},{1,5},{2,6},{3,7},{4,0},{5,1},{6,2},{7,3},{8,12},{9,13},{10,... | collective-permute-start | bytes 294920 | tf_op jit(solution)/shard_map/ppermute | solution.py:308
  8.5 1.6 %collective-permute-start.2 = (bf16[2,16,1536]{2,1,0:T(8,128)(2,1)S(1)}, bf16[2,16,1536]{2,1,0:T(8,128)(2,1)S(1)}, u32[]{:S(2)}, u32[]{:S(2)}) collective-permute-start(bf16[2,16,1536]{2,1,0:T(8,128)(2,1)S(1)} %get-tuple-element.17), channel_id=1, source_target_pairs={{0,2},{1,3},{2,0},{3,1},{4,6},{5,7},{6,4},{7,5},{8,10},{9,11},{10,... | collective-permute-start | bytes 294920 | tf_op jit(solution)/shard_map/ppermute | solution.py:308
  10.1 0.0 collective-permute-start.3
  10.1 1.5 %start.1 = (f32[2,128,128]{2,1,0:T(8,128)S(1)}, f32[64,128]{1,0:T(8,128)S(1)}) custom-call(f32[16,2,16,32]{3,2,1,0:T(8,128)} %bitcast.24, bf16[2,16,1536]{2,1,0:T(8,128)(2,1)S(1)} %get-tuple-element.13._), custom_call_target="tpu_custom_call" | custom-call | tf_op jit(solution)/shard_map/start/pallas_call | solution.py:340
  11.6 2.8 %collective-permute-done = bf16[2,16,1536]{2,1,0:T(8,128)(2,1)S(1)} collective-permute-done((bf16[2,16,1536]{2,1,0:T(8,128)(2,1)S(1)}, bf16[2,16,1536]{2,1,0:T(8,128)(2,1)S(1)}, u32[]{:S(2)}, u32[]{:S(2)}) %collective-permute-start) | collective-permute-done | bytes 98336 | tf_op jit(solution)/shard_map/ppermute | solution.py:308
  14.5 0.1 collective-permute-start.1
  14.5 0.0 collective-permute-done.2
  14.6 2.1 %collective-permute-done.3 = bf16[2,16,1536]{2,1,0:T(8,128)(2,1)S(1)} collective-permute-done((bf16[2,16,1536]{2,1,0:T(8,128)(2,1)S(1)}, bf16[2,16,1536]{2,1,0:T(8,128)(2,1)S(1)}, u32[]{:S(2)}, u32[]{:S(2)}) %collective-permute-start.3) | collective-permute-done | bytes 98336 | tf_op jit(solution)/shard_map/ppermute | solution.py:308
  16.7 0.1 collective-permute-start.4
  16.8 0.0 collective-permute-done.1
  16.8 1.3 %collective-permute-done.4 = bf16[2,16,1536]{2,1,0:T(8,128)(2,1)S(1)} collective-permute-done((bf16[2,16,1536]{2,1,0:T(8,128)(2,1)S(1)}, bf16[2,16,1536]{2,1,0:T(8,128)(2,1)S(1)}, u32[]{:S(2)}, u32[]{:S(2)}) %collective-permute-start.4) | collective-permute-done | bytes 98336 | tf_op jit(solution)/shard_map/ppermute | solution.py:308
  18.1 0.3 gram.1.refs_0_
  18.4 2.5 %collective-permute-start.7 = (f32[32,128]{1,0:T(8,128)S(1)}, f32[32,128]{1,0:T(8,128)S(1)}, u32[]{:S(2)}, u32[]{:S(2)}) collective-permute-start(f32[32,128]{1,0:T(8,128)S(1)} %gram.1.refs_0_), channel_id=1, source_target_pairs={{0,24},{8,16},{16,8},{24,0},{1,25},{9,17},{17,9},{25,1},{2,26},{10... | collective-permute-start | bytes 49160 | tf_op jit(solution)/shard_map/ppermute | solution.py:308
  20.9 0.5 %collective-permute-start.6 = (f32[32,128]{1,0:T(8,128)S(1)}, f32[32,128]{1,0:T(8,128)S(1)}, u32[]{:S(2)}, u32[]{:S(2)}) collective-permute-start(f32[32,128]{1,0:T(8,128)S(1)} %gram.1.refs_0_), channel_id=1, source_target_pairs={{0,16},{8,24},{16,0},{24,8},{1,17},{9,25},{17,1},{25,9},{2,18},{10... | collective-permute-start | bytes 49160 | tf_op jit(solution)/shard_map/ppermute | solution.py:308
  21.4 0.6 %collective-permute-start.5 = (f32[32,128]{1,0:T(8,128)S(1)}, f32[32,128]{1,0:T(8,128)S(1)}, u32[]{:S(2)}, u32[]{:S(2)}) collective-permute-start(f32[32,128]{1,0:T(8,128)S(1)} %gram.1.refs_0_), channel_id=1, source_target_pairs={{0,8},{8,0},{16,24},{24,16},{1,9},{9,1},{17,25},{25,17},{2,10},{10... | collective-permute-start | bytes 49160 | tf_op jit(solution)/shard_map/ppermute | solution.py:308
  22.0 1.1 %collective-permute-done.7.refs_3_ = f32[32,128]{1,0:T(8,128)S(1)} collective-permute-done((f32[32,128]{1,0:T(8,128)S(1)}, f32[32,128]{1,0:T(8,128)S(1)}, u32[]{:S(2)}, u32[]{:S(2)}) %collective-permute-start.7) | collective-permute-done | bytes 16416 | tf_op jit(solution)/shard_map/ppermute | solution.py:308
  23.1 1.5 %collective-permute-done.6.refs_2_ = f32[32,128]{1,0:T(8,128)S(1)} collective-permute-done((f32[32,128]{1,0:T(8,128)S(1)}, f32[32,128]{1,0:T(8,128)S(1)}, u32[]{:S(2)}, u32[]{:S(2)}) %collective-permute-start.6) | collective-permute-done | bytes 16416 | tf_op jit(solution)/shard_map/ppermute | solution.py:308
  24.6 0.5 %collective-permute-done.5.refs_1_ = f32[32,128]{1,0:T(8,128)S(1)} collective-permute-done((f32[32,128]{1,0:T(8,128)S(1)}, f32[32,128]{1,0:T(8,128)S(1)}, u32[]{:S(2)}, u32[]{:S(2)}) %collective-permute-start.5) | collective-permute-done | bytes 16416 | tf_op jit(solution)/shard_map/ppermute | solution.py:308
  25.1 8.3 %subspace.1 = (bf16[64,128]{1,0:T(8,128)(2,1)S(1)}, f32[16,16]{1,0:T(8,128)S(1)}) custom-call(f32[32,128]{1,0:T(8,128)S(1)} %gram.1.refs_0_, f32[32,128]{1,0:T(8,128)S(1)} %collective-permute-done.5.refs_1_, f32[32,128]{1,0:T(8,128)S(1)} %collective-permute-done.6.refs_2_, f32[32,128]{1,0:T(8,128)S(1)} %collective-permute-done.7.refs_3_, ...), custom_call_target="tpu_custom_call" | custom-call | tf_op jit(solution)/shard_map/subspace/pallas_call | solution.py:372
  33.4 0.1 collective-permute-start.8
  33.5 1.2 %collective-permute-done.8 = f32[16,16]{1,0:T(8,128)S(1)} collective-permute-done((f32[16,16]{1,0:T(8,128)S(1)}, f32[16,16]{1,0:T(8,128)S(1)}, u32[]{:S(2)}, u32[]{:S(2)}) %collective-permute-start.8) | collective-permute-done | bytes 1056 | tf_op jit(solution)/shard_map/ppermute | solution.py:308
  34.6 2.6 %collective-permute-start.11 = (f32[16,16]{1,0:T(8,128)S(1)}, f32[16,16]{1,0:T(8,128)S(1)}, u32[]{:S(2)}, u32[]{:S(2)}) collective-permute-start(f32[16,16]{1,0:T(8,128)S(1)} %add.12), channel_id=1, source_target_pairs={{0,6},{1,7},{2,4},{3,5},{4,2},{5,3},{6,0},{7,1},{8,14},{9,15},{10,... | collective-permute-start | bytes 3080 | tf_op jit(solution)/shard_map/ppermute | solution.py:308
  37.2 1.1 %collective-permute-start.10 = (f32[16,16]{1,0:T(8,128)S(1)}, f32[16,16]{1,0:T(8,128)S(1)}, u32[]{:S(2)}, u32[]{:S(2)}) collective-permute-start(f32[16,16]{1,0:T(8,128)S(1)} %add.12), channel_id=1, source_target_pairs={{0,4},{1,5},{2,6},{3,7},{4,0},{5,1},{6,2},{7,3},{8,12},{9,13},{10,... | collective-permute-start | bytes 3080 | tf_op jit(solution)/shard_map/ppermute | solution.py:308
  38.3 0.8 %collective-permute-start.9 = (f32[16,16]{1,0:T(8,128)S(1)}, f32[16,16]{1,0:T(8,128)S(1)}, u32[]{:S(2)}, u32[]{:S(2)}) collective-permute-start(f32[16,16]{1,0:T(8,128)S(1)} %add.12), channel_id=1, source_target_pairs={{0,2},{1,3},{2,0},{3,1},{4,6},{5,7},{6,4},{7,5},{8,10},{9,11},{10,... | collective-permute-start | bytes 3080 | tf_op jit(solution)/shard_map/ppermute | solution.py:308
  39.0 0.0 copy-done
  39.0 0.9 %modes.1 = f32[2,2,3,16,512]{4,3,2,1,0:T(8,128)} custom-call(f32[1,512]{1,0:T(1,128)S(1)} %bitcast.21, bf16[64,128]{1,0:T(8,128)(2,1)S(1)} %get-tuple-element.22.coef, bf16[16,1536]{1,0:T(8,128)(2,1)S(1)} %get-tuple-element.35.refs_0_, bf16[16,1536]{1,0:T(8,128)(2,1)S(1)} %get-tuple-element.29.refs_1_, bf16[16,1536]{1,0:T(8,128)(2,1)S(1)} %get-tuple-element.33.refs_2_, ...), custom_call_target="tpu_custom_call" | custom-call | tf_op jit(solution)/shard_map/modes/pallas_call | solution.py:382
  40.0 0.1 collective-permute-done.11
  40.1 1.7 %collective-permute-done.10 = f32[16,16]{1,0:T(8,128)S(1)} collective-permute-done((f32[16,16]{1,0:T(8,128)S(1)}, f32[16,16]{1,0:T(8,128)S(1)}, u32[]{:S(2)}, u32[]{:S(2)}) %collective-permute-start.10) | collective-permute-done | bytes 1056 | tf_op jit(solution)/shard_map/ppermute | solution.py:308
  41.8 0.1 collective-permute-done.9
  41.9 0.6 %add_add_fusion = f32[16,16]{1,0:T(8,128)} fusion(f32[16,16]{1,0:T(8,128)S(1)} %collective-permute-done.11, f32[16,16]{1,0:T(8,128)S(1)} %collective-permute-done.10, f32[16,16]{1,0:T(8,128)S(1)} %add.12, f32[16,16]{1,0:T(8,128)S(1)} %collective-permute-done.9), kind=kLoop, calls=%fused_computation.10 | loop fusion | flops 768 | bytes 5120 | tf_op jit(solution)/shard_map/add | solution.py:392
  (9 shorter events, 0.1 us)
Async XLA Ops:
  0.6 38.4 %copy-start = (f32[512]{0:T(512)S(1)}, f32[512]{0:T(512)}, u32[]{:S(2)}) copy-start(f32[512]{0:T(512)} %param.5) | copy-start | bytes 6148
  4.4 10.0 %collective-permute-start = (bf16[2,16,1536]{2,1,0:T(8,128)(2,1)S(1)}, bf16[2,16,1536]{2,1,0:T(8,128)(2,1)S(1)}, u32[]{:S(2)}, u32[]{:S(2)}) collective-permute-start(bf16[2,16,1536]{2,1,0:T(8,128)(2,1)S(1)} %get-tuple-element.14), channel_id=1, source_target_pairs={{0,4},{1,5},{2,6},{3,7},{4,0},{5,1},{6,2},{7,3},{8,12},{9,13},{10,... | collective-permute-start | bytes 294920 | tf_op jit(solution)/shard_map/ppermute | solution.py:308
  8.5 6.1 %collective-permute-start.2 = (bf16[2,16,1536]{2,1,0:T(8,128)(2,1)S(1)}, bf16[2,16,1536]{2,1,0:T(8,128)(2,1)S(1)}, u32[]{:S(2)}, u32[]{:S(2)}) collective-permute-start(bf16[2,16,1536]{2,1,0:T(8,128)(2,1)S(1)} %get-tuple-element.17), channel_id=1, source_target_pairs={{0,2},{1,3},{2,0},{3,1},{4,6},{5,7},{6,4},{7,5},{8,10},{9,11},{10,... | collective-permute-start | bytes 294920 | tf_op jit(solution)/shard_map/ppermute | solution.py:308
  10.1 6.6 %collective-permute-start.3 = (bf16[2,16,1536]{2,1,0:T(8,128)(2,1)S(1)}, bf16[2,16,1536]{2,1,0:T(8,128)(2,1)S(1)}, u32[]{:S(2)}, u32[]{:S(2)}) collective-permute-start(bf16[2,16,1536]{2,1,0:T(8,128)(2,1)S(1)} %get-tuple-element.19), channel_id=1, source_target_pairs={{0,6},{1,7},{2,4},{3,5},{4,2},{5,3},{6,0},{7,1},{8,14},{9,15},{10,... | collective-permute-start | bytes 294920 | tf_op jit(solution)/shard_map/ppermute | solution.py:308
  14.5 2.3 %collective-permute-start.1 = (bf16[2,16,1536]{2,1,0:T(8,128)(2,1)S(1)}, bf16[2,16,1536]{2,1,0:T(8,128)(2,1)S(1)}, u32[]{:S(2)}, u32[]{:S(2)}) collective-permute-start(bf16[2,16,1536]{2,1,0:T(8,128)(2,1)S(1)} %pad_maximum_fusion), channel_id=1, source_target_pairs={{0,1},{1,0},{2,3},{3,2},{4,5},{5,4},{6,7},{7,6},{8,9},{9,8},{10,11... | collective-permute-start | bytes 294920 | tf_op jit(solution)/shard_map/ppermute | solution.py:308
  16.7 1.4 %collective-permute-start.4 = (bf16[2,16,1536]{2,1,0:T(8,128)(2,1)S(1)}, bf16[2,16,1536]{2,1,0:T(8,128)(2,1)S(1)}, u32[]{:S(2)}, u32[]{:S(2)}) collective-permute-start(bf16[2,16,1536]{2,1,0:T(8,128)(2,1)S(1)} %pad_maximum_fusion.1), channel_id=1, source_target_pairs={{0,1},{1,0},{2,3},{3,2},{4,5},{5,4},{6,7},{7,6},{8,9},{9,8},{10,11... | collective-permute-start | bytes 294920 | tf_op jit(solution)/shard_map/ppermute | solution.py:308
  18.4 4.7 %collective-permute-start.7 = (f32[32,128]{1,0:T(8,128)S(1)}, f32[32,128]{1,0:T(8,128)S(1)}, u32[]{:S(2)}, u32[]{:S(2)}) collective-permute-start(f32[32,128]{1,0:T(8,128)S(1)} %gram.1.refs_0_), channel_id=1, source_target_pairs={{0,24},{8,16},{16,8},{24,0},{1,25},{9,17},{17,9},{25,1},{2,26},{10... | collective-permute-start | bytes 49160 | tf_op jit(solution)/shard_map/ppermute | solution.py:308
  20.9 3.7 %collective-permute-start.6 = (f32[32,128]{1,0:T(8,128)S(1)}, f32[32,128]{1,0:T(8,128)S(1)}, u32[]{:S(2)}, u32[]{:S(2)}) collective-permute-start(f32[32,128]{1,0:T(8,128)S(1)} %gram.1.refs_0_), channel_id=1, source_target_pairs={{0,16},{8,24},{16,0},{24,8},{1,17},{9,25},{17,1},{25,9},{2,18},{10... | collective-permute-start | bytes 49160 | tf_op jit(solution)/shard_map/ppermute | solution.py:308
  21.4 3.7 %collective-permute-start.5 = (f32[32,128]{1,0:T(8,128)S(1)}, f32[32,128]{1,0:T(8,128)S(1)}, u32[]{:S(2)}, u32[]{:S(2)}) collective-permute-start(f32[32,128]{1,0:T(8,128)S(1)} %gram.1.refs_0_), channel_id=1, source_target_pairs={{0,8},{8,0},{16,24},{24,16},{1,9},{9,1},{17,25},{25,17},{2,10},{10... | collective-permute-start | bytes 49160 | tf_op jit(solution)/shard_map/ppermute | solution.py:308
  33.4 1.2 %collective-permute-start.8 = (f32[16,16]{1,0:T(8,128)S(1)}, f32[16,16]{1,0:T(8,128)S(1)}, u32[]{:S(2)}, u32[]{:S(2)}) collective-permute-start(f32[16,16]{1,0:T(8,128)S(1)} %get-tuple-element.23), channel_id=1, source_target_pairs={{0,1},{1,0},{2,3},{3,2},{4,5},{5,4},{6,7},{7,6},{8,9},{9,8},{10,11... | collective-permute-start | bytes 3080 | tf_op jit(solution)/shard_map/ppermute | solution.py:308
  34.6 5.4 %collective-permute-start.11 = (f32[16,16]{1,0:T(8,128)S(1)}, f32[16,16]{1,0:T(8,128)S(1)}, u32[]{:S(2)}, u32[]{:S(2)}) collective-permute-start(f32[16,16]{1,0:T(8,128)S(1)} %add.12), channel_id=1, source_target_pairs={{0,6},{1,7},{2,4},{3,5},{4,2},{5,3},{6,0},{7,1},{8,14},{9,15},{10,... | collective-permute-start | bytes 3080 | tf_op jit(solution)/shard_map/ppermute | solution.py:308
  37.2 4.6 %collective-permute-start.10 = (f32[16,16]{1,0:T(8,128)S(1)}, f32[16,16]{1,0:T(8,128)S(1)}, u32[]{:S(2)}, u32[]{:S(2)}) collective-permute-start(f32[16,16]{1,0:T(8,128)S(1)} %add.12), channel_id=1, source_target_pairs={{0,4},{1,5},{2,6},{3,7},{4,0},{5,1},{6,2},{7,3},{8,12},{9,13},{10,... | collective-permute-start | bytes 3080 | tf_op jit(solution)/shard_map/ppermute | solution.py:308
  38.3 3.7 %collective-permute-start.9 = (f32[16,16]{1,0:T(8,128)S(1)}, f32[16,16]{1,0:T(8,128)S(1)}, u32[]{:S(2)}, u32[]{:S(2)}) collective-permute-start(f32[16,16]{1,0:T(8,128)S(1)} %add.12), channel_id=1, source_target_pairs={{0,2},{1,3},{2,0},{3,1},{4,6},{5,7},{6,4},{7,5},{8,10},{9,11},{10,... | collective-permute-start | bytes 3080 | tf_op jit(solution)/shard_map/ppermute | solution.py:308

commit v6 on v5

--- a/solution.py
+++ b/solution.py
@@ -70,7 +70,7 @@
     table_copy.start()
     quad_copy.start()
     for i, copy in enumerate(copies[:IN_FLIGHT]):
-        copy.start(priority=int(i < blocks))
+        copy.start(priority=int(i < 6))
     me = lax.axis_index("blk")
     height = piles.shape[1]
     table_copy.wait()

time: 42.7 us -> 42.5 us (level)
  transfers between devices with their start and end apart: 12 -> 12, of which waited for: 10 -> 9; matrix products, arithmetic and copies ran while one was open for 0% -> 0% of each run, Pallas kernels for 6% -> 6%
where the time goes in v6:
time: 42.5 us; the launch traced here: 42.3 us
  Pallas kernels  14.6 us (34%)
  starting transfers between devices  13.8 us (32%)
  waiting for transfers between devices  12.5 us (29%)
  between operations  0.76 us (2%)
  other arithmetic  0.63 us (1%)
    ppermute x12, starting transfers between devices, exchange(): return lax.ppermute(array, axis, [(i, i ^ distance) for i in range(size)])  13.8 us
    ppermute x12, waiting for transfers between devices, exchange(): return lax.ppermute(array, axis, [(i, i ^ distance) for i in range(size)])  12.5 us
    pallas_call x1, Pallas kernels, per_device(): call(functools.partial(subspace_kernel, share, blocks, width * spaces, le...  8.27 us
    pallas_call x1, Pallas kernels, per_device(): call(functools.partial(spectra_kernel, groups), [jax.ShapeDtypeStruct((2,...  3.46 us
    pallas_call x1, Pallas kernels, per_device(): call(functools.partial(start_kernel, share, blocks), [jax.ShapeDtypeStruc...  1.54 us
    pallas_call x1, Pallas kernels, per_device(): call(functools.partial(modes_kernel, share), jax.ShapeDtypeStruct((share,...  0.95 us
  transfers between devices with their start and end apart: 12, of which 9 were waited for; matrix products, arithmetic and copies ran while one was open for 0% of the time, Pallas kernels for 6%

profile of v6, /device:TPU:0, one launch (start us, length us, event | category | flops | bytes accessed | tf_op | source)
XLA Modules:
  0.0 42.3 jit_solution(8623273446239804083)
XLA Ops:
  0.6 0.0 copy-start
  0.6 3.5 %spectra.1 = (bf16[2,16,1536]{2,1,0:T(8,128)(2,1)S(1)}, bf16[2,16,1536]{2,1,0:T(8,128)(2,1)S(1)}, bf16[2,16,1536]{2,1,0:T(8,128)(2,1)S(1)}, bf16[2,16,1536]{2,1,0:T(8,128)(2,1)S(1)}) custom-call(bf16[4,3,512,512]{3,2,1,0:T(8,128)(2,1)} %bitcast.22, bf16[32,512]{1,0:T(8,128)(2,1)} %constant.2.clone.table_hbm, f32[1,512]{1,0:T(1,128)} %bitcast.20), custom_call_target="tpu_custom_call" | custom-call | tf_op jit(solution)/shard_map/spectra/pallas_call | solution.py:324
  4.1 4.1 %collective-permute-start = (bf16[2,16,1536]{2,1,0:T(8,128)(2,1)S(1)}, bf16[2,16,1536]{2,1,0:T(8,128)(2,1)S(1)}, u32[]{:S(2)}, u32[]{:S(2)}) collective-permute-start(bf16[2,16,1536]{2,1,0:T(8,128)(2,1)S(1)} %get-tuple-element.14), channel_id=1, source_target_pairs={{0,4},{1,5},{2,6},{3,7},{4,0},{5,1},{6,2},{7,3},{8,12},{9,13},{10,... | collective-permute-start | bytes 294920 | tf_op jit(solution)/shard_map/ppermute | solution.py:308
  8.2 1.6 %collective-permute-start.2 = (bf16[2,16,1536]{2,1,0:T(8,128)(2,1)S(1)}, bf16[2,16,1536]{2,1,0:T(8,128)(2,1)S(1)}, u32[]{:S(2)}, u32[]{:S(2)}) collective-permute-start(bf16[2,16,1536]{2,1,0:T(8,128)(2,1)S(1)} %get-tuple-element.17), channel_id=1, source_target_pairs={{0,2},{1,3},{2,0},{3,1},{4,6},{5,7},{6,4},{7,5},{8,10},{9,11},{10,... | collective-permute-start | bytes 294920 | tf_op jit(solution)/shard_map/ppermute | solution.py:308
  9.8 0.0 collective-permute-start.3
  9.8 1.5 %start.1 = (f32[2,128,128]{2,1,0:T(8,128)S(1)}, f32[64,128]{1,0:T(8,128)S(1)}) custom-call(f32[16,2,16,32]{3,2,1,0:T(8,128)} %bitcast.24, bf16[2,16,1536]{2,1,0:T(8,128)(2,1)S(1)} %get-tuple-element.13._), custom_call_target="tpu_custom_call" | custom-call | tf_op jit(solution)/shard_map/start/pallas_call | solution.py:340
  11.4 2.8 %collective-permute-done = bf16[2,16,1536]{2,1,0:T(8,128)(2,1)S(1)} collective-permute-done((bf16[2,16,1536]{2,1,0:T(8,128)(2,1)S(1)}, bf16[2,16,1536]{2,1,0:T(8,128)(2,1)S(1)}, u32[]{:S(2)}, u32[]{:S(2)}) %collective-permute-start) | collective-permute-done | bytes 98336 | tf_op jit(solution)/shard_map/ppermute | solution.py:308
  14.2 0.1 collective-permute-start.1
  14.3 0.0 collective-permute-done.2
  14.3 2.1 %collective-permute-done.3 = bf16[2,16,1536]{2,1,0:T(8,128)(2,1)S(1)} collective-permute-done((bf16[2,16,1536]{2,1,0:T(8,128)(2,1)S(1)}, bf16[2,16,1536]{2,1,0:T(8,128)(2,1)S(1)}, u32[]{:S(2)}, u32[]{:S(2)}) %collective-permute-start.3) | collective-permute-done | bytes 98336 | tf_op jit(solution)/shard_map/ppermute | solution.py:308
  16.4 0.1 collective-permute-start.4
  16.5 0.0 collective-permute-done.1
  16.5 1.3 %collective-permute-done.4 = bf16[2,16,1536]{2,1,0:T(8,128)(2,1)S(1)} collective-permute-done((bf16[2,16,1536]{2,1,0:T(8,128)(2,1)S(1)}, bf16[2,16,1536]{2,1,0:T(8,128)(2,1)S(1)}, u32[]{:S(2)}, u32[]{:S(2)}) %collective-permute-start.4) | collective-permute-done | bytes 98336 | tf_op jit(solution)/shard_map/ppermute | solution.py:308
  17.8 0.3 gram.1.refs_0_
  18.1 2.5 %collective-permute-start.7 = (f32[32,128]{1,0:T(8,128)S(1)}, f32[32,128]{1,0:T(8,128)S(1)}, u32[]{:S(2)}, u32[]{:S(2)}) collective-permute-start(f32[32,128]{1,0:T(8,128)S(1)} %gram.1.refs_0_), channel_id=1, source_target_pairs={{0,24},{8,16},{16,8},{24,0},{1,25},{9,17},{17,9},{25,1},{2,26},{10... | collective-permute-start | bytes 49160 | tf_op jit(solution)/shard_map/ppermute | solution.py:308
  20.6 0.5 %collective-permute-start.6 = (f32[32,128]{1,0:T(8,128)S(1)}, f32[32,128]{1,0:T(8,128)S(1)}, u32[]{:S(2)}, u32[]{:S(2)}) collective-permute-start(f32[32,128]{1,0:T(8,128)S(1)} %gram.1.refs_0_), channel_id=1, source_target_pairs={{0,16},{8,24},{16,0},{24,8},{1,17},{9,25},{17,1},{25,9},{2,18},{10... | collective-permute-start | bytes 49160 | tf_op jit(solution)/shard_map/ppermute | solution.py:308
  21.1 0.6 %collective-permute-start.5 = (f32[32,128]{1,0:T(8,128)S(1)}, f32[32,128]{1,0:T(8,128)S(1)}, u32[]{:S(2)}, u32[]{:S(2)}) collective-permute-start(f32[32,128]{1,0:T(8,128)S(1)} %gram.1.refs_0_), channel_id=1, source_target_pairs={{0,8},{8,0},{16,24},{24,16},{1,9},{9,1},{17,25},{25,17},{2,10},{10... | collective-permute-start | bytes 49160 | tf_op jit(solution)/shard_map/ppermute | solution.py:308
  21.7 1.1 %collective-permute-done.7.refs_3_ = f32[32,128]{1,0:T(8,128)S(1)} collective-permute-done((f32[32,128]{1,0:T(8,128)S(1)}, f32[32,128]{1,0:T(8,128)S(1)}, u32[]{:S(2)}, u32[]{:S(2)}) %collective-permute-start.7) | collective-permute-done | bytes 16416 | tf_op jit(solution)/shard_map/ppermute | solution.py:308
  22.8 1.5 %collective-permute-done.6.refs_2_ = f32[32,128]{1,0:T(8,128)S(1)} collective-permute-done((f32[32,128]{1,0:T(8,128)S(1)}, f32[32,128]{1,0:T(8,128)S(1)}, u32[]{:S(2)}, u32[]{:S(2)}) %collective-permute-start.6) | collective-permute-done | bytes 16416 | tf_op jit(solution)/shard_map/ppermute | solution.py:308
  24.3 0.5 %collective-permute-done.5.refs_1_ = f32[32,128]{1,0:T(8,128)S(1)} collective-permute-done((f32[32,128]{1,0:T(8,128)S(1)}, f32[32,128]{1,0:T(8,128)S(1)}, u32[]{:S(2)}, u32[]{:S(2)}) %collective-permute-start.5) | collective-permute-done | bytes 16416 | tf_op jit(solution)/shard_map/ppermute | solution.py:308
  24.9 8.3 %subspace.1 = (bf16[64,128]{1,0:T(8,128)(2,1)S(1)}, f32[16,16]{1,0:T(8,128)S(1)}) custom-call(f32[32,128]{1,0:T(8,128)S(1)} %gram.1.refs_0_, f32[32,128]{1,0:T(8,128)S(1)} %collective-permute-done.5.refs_1_, f32[32,128]{1,0:T(8,128)S(1)} %collective-permute-done.6.refs_2_, f32[32,128]{1,0:T(8,128)S(1)} %collective-permute-done.7.refs_3_, ...), custom_call_target="tpu_custom_call" | custom-call | tf_op jit(solution)/shard_map/subspace/pallas_call | solution.py:372
  33.1 0.1 collective-permute-start.8
  33.2 1.2 %collective-permute-done.8 = f32[16,16]{1,0:T(8,128)S(1)} collective-permute-done((f32[16,16]{1,0:T(8,128)S(1)}, f32[16,16]{1,0:T(8,128)S(1)}, u32[]{:S(2)}, u32[]{:S(2)}) %collective-permute-start.8) | collective-permute-done | bytes 1056 | tf_op jit(solution)/shard_map/ppermute | solution.py:308
  34.4 2.8 %collective-permute-start.11 = (f32[16,16]{1,0:T(8,128)S(1)}, f32[16,16]{1,0:T(8,128)S(1)}, u32[]{:S(2)}, u32[]{:S(2)}) collective-permute-start(f32[16,16]{1,0:T(8,128)S(1)} %add.12), channel_id=1, source_target_pairs={{0,6},{1,7},{2,4},{3,5},{4,2},{5,3},{6,0},{7,1},{8,14},{9,15},{10,... | collective-permute-start | bytes 3080 | tf_op jit(solution)/shard_map/ppermute | solution.py:308
  37.2 0.8 %collective-permute-start.10 = (f32[16,16]{1,0:T(8,128)S(1)}, f32[16,16]{1,0:T(8,128)S(1)}, u32[]{:S(2)}, u32[]{:S(2)}) collective-permute-start(f32[16,16]{1,0:T(8,128)S(1)} %add.12), channel_id=1, source_target_pairs={{0,4},{1,5},{2,6},{3,7},{4,0},{5,1},{6,2},{7,3},{8,12},{9,13},{10,... | collective-permute-start | bytes 3080 | tf_op jit(solution)/shard_map/ppermute | solution.py:308
  38.0 0.8 %collective-permute-start.9 = (f32[16,16]{1,0:T(8,128)S(1)}, f32[16,16]{1,0:T(8,128)S(1)}, u32[]{:S(2)}, u32[]{:S(2)}) collective-permute-start(f32[16,16]{1,0:T(8,128)S(1)} %add.12), channel_id=1, source_target_pairs={{0,2},{1,3},{2,0},{3,1},{4,6},{5,7},{6,4},{7,5},{8,10},{9,11},{10,... | collective-permute-start | bytes 3080 | tf_op jit(solution)/shard_map/ppermute | solution.py:308
  38.8 0.0 copy-done
  38.8 0.9 %modes.1 = f32[2,2,3,16,512]{4,3,2,1,0:T(8,128)} custom-call(f32[1,512]{1,0:T(1,128)S(1)} %bitcast.21, bf16[64,128]{1,0:T(8,128)(2,1)S(1)} %get-tuple-element.22.coef, bf16[16,1536]{1,0:T(8,128)(2,1)S(1)} %get-tuple-element.35.refs_0_, bf16[16,1536]{1,0:T(8,128)(2,1)S(1)} %get-tuple-element.29.refs_1_, bf16[16,1536]{1,0:T(8,128)(2,1)S(1)} %get-tuple-element.33.refs_2_, ...), custom_call_target="tpu_custom_call" | custom-call | tf_op jit(solution)/shard_map/modes/pallas_call | solution.py:382
  39.7 0.1 collective-permute-done.11
  39.8 1.9 %collective-permute-done.10 = f32[16,16]{1,0:T(8,128)S(1)} collective-permute-done((f32[16,16]{1,0:T(8,128)S(1)}, f32[16,16]{1,0:T(8,128)S(1)}, u32[]{:S(2)}, u32[]{:S(2)}) %collective-permute-start.10) | collective-permute-done | bytes 1056 | tf_op jit(solution)/shard_map/ppermute | solution.py:308
  41.7 0.0 collective-permute-done.9
  41.7 0.6 %add_add_fusion = f32[16,16]{1,0:T(8,128)} fusion(f32[16,16]{1,0:T(8,128)S(1)} %collective-permute-done.11, f32[16,16]{1,0:T(8,128)S(1)} %collective-permute-done.10, f32[16,16]{1,0:T(8,128)S(1)} %add.12, f32[16,16]{1,0:T(8,128)S(1)} %collective-permute-done.9), kind=kLoop, calls=%fused_computation.10 | loop fusion | flops 768 | bytes 5120 | tf_op jit(solution)/shard_map/add | solution.py:392
  (9 shorter events, 0.1 us)
Async XLA Ops:
  0.6 38.1 %copy-start = (f32[512]{0:T(512)S(1)}, f32[512]{0:T(512)}, u32[]{:S(2)}) copy-start(f32[512]{0:T(512)} %param.5) | copy-start | bytes 6148
  4.1 10.0 %collective-permute-start = (bf16[2,16,1536]{2,1,0:T(8,128)(2,1)S(1)}, bf16[2,16,1536]{2,1,0:T(8,128)(2,1)S(1)}, u32[]{:S(2)}, u32[]{:S(2)}) collective-permute-start(bf16[2,16,1536]{2,1,0:T(8,128)(2,1)S(1)} %get-tuple-element.14), channel_id=1, source_target_pairs={{0,4},{1,5},{2,6},{3,7},{4,0},{5,1},{6,2},{7,3},{8,12},{9,13},{10,... | collective-permute-start | bytes 294920 | tf_op jit(solution)/shard_map/ppermute | solution.py:308
  8.2 6.1 %collective-permute-start.2 = (bf16[2,16,1536]{2,1,0:T(8,128)(2,1)S(1)}, bf16[2,16,1536]{2,1,0:T(8,128)(2,1)S(1)}, u32[]{:S(2)}, u32[]{:S(2)}) collective-permute-start(bf16[2,16,1536]{2,1,0:T(8,128)(2,1)S(1)} %get-tuple-element.17), channel_id=1, source_target_pairs={{0,2},{1,3},{2,0},{3,1},{4,6},{5,7},{6,4},{7,5},{8,10},{9,11},{10,... | collective-permute-start | bytes 294920 | tf_op jit(solution)/shard_map/ppermute | solution.py:308
  9.8 6.6 %collective-permute-start.3 = (bf16[2,16,1536]{2,1,0:T(8,128)(2,1)S(1)}, bf16[2,16,1536]{2,1,0:T(8,128)(2,1)S(1)}, u32[]{:S(2)}, u32[]{:S(2)}) collective-permute-start(bf16[2,16,1536]{2,1,0:T(8,128)(2,1)S(1)} %get-tuple-element.19), channel_id=1, source_target_pairs={{0,6},{1,7},{2,4},{3,5},{4,2},{5,3},{6,0},{7,1},{8,14},{9,15},{10,... | collective-permute-start | bytes 294920 | tf_op jit(solution)/shard_map/ppermute | solution.py:308
  14.2 2.3 %collective-permute-start.1 = (bf16[2,16,1536]{2,1,0:T(8,128)(2,1)S(1)}, bf16[2,16,1536]{2,1,0:T(8,128)(2,1)S(1)}, u32[]{:S(2)}, u32[]{:S(2)}) collective-permute-start(bf16[2,16,1536]{2,1,0:T(8,128)(2,1)S(1)} %pad_maximum_fusion), channel_id=1, source_target_pairs={{0,1},{1,0},{2,3},{3,2},{4,5},{5,4},{6,7},{7,6},{8,9},{9,8},{10,11... | collective-permute-start | bytes 294920 | tf_op jit(solution)/shard_map/ppermute | solution.py:308
  16.4 1.4 %collective-permute-start.4 = (bf16[2,16,1536]{2,1,0:T(8,128)(2,1)S(1)}, bf16[2,16,1536]{2,1,0:T(8,128)(2,1)S(1)}, u32[]{:S(2)}, u32[]{:S(2)}) collective-permute-start(bf16[2,16,1536]{2,1,0:T(8,128)(2,1)S(1)} %pad_maximum_fusion.1), channel_id=1, source_target_pairs={{0,1},{1,0},{2,3},{3,2},{4,5},{5,4},{6,7},{7,6},{8,9},{9,8},{10,11... | collective-permute-start | bytes 294920 | tf_op jit(solution)/shard_map/ppermute | solution.py:308
  18.1 4.7 %collective-permute-start.7 = (f32[32,128]{1,0:T(8,128)S(1)}, f32[32,128]{1,0:T(8,128)S(1)}, u32[]{:S(2)}, u32[]{:S(2)}) collective-permute-start(f32[32,128]{1,0:T(8,128)S(1)} %gram.1.refs_0_), channel_id=1, source_target_pairs={{0,24},{8,16},{16,8},{24,0},{1,25},{9,17},{17,9},{25,1},{2,26},{10... | collective-permute-start | bytes 49160 | tf_op jit(solution)/shard_map/ppermute | solution.py:308
  20.6 3.7 %collective-permute-start.6 = (f32[32,128]{1,0:T(8,128)S(1)}, f32[32,128]{1,0:T(8,128)S(1)}, u32[]{:S(2)}, u32[]{:S(2)}) collective-permute-start(f32[32,128]{1,0:T(8,128)S(1)} %gram.1.refs_0_), channel_id=1, source_target_pairs={{0,16},{8,24},{16,0},{24,8},{1,17},{9,25},{17,1},{25,9},{2,18},{10... | collective-permute-start | bytes 49160 | tf_op jit(solution)/shard_map/ppermute | solution.py:308
  21.1 3.7 %collective-permute-start.5 = (f32[32,128]{1,0:T(8,128)S(1)}, f32[32,128]{1,0:T(8,128)S(1)}, u32[]{:S(2)}, u32[]{:S(2)}) collective-permute-start(f32[32,128]{1,0:T(8,128)S(1)} %gram.1.refs_0_), channel_id=1, source_target_pairs={{0,8},{8,0},{16,24},{24,16},{1,9},{9,1},{17,25},{25,17},{2,10},{10... | collective-permute-start | bytes 49160 | tf_op jit(solution)/shard_map/ppermute | solution.py:308
  33.1 1.2 %collective-permute-start.8 = (f32[16,16]{1,0:T(8,128)S(1)}, f32[16,16]{1,0:T(8,128)S(1)}, u32[]{:S(2)}, u32[]{:S(2)}) collective-permute-start(f32[16,16]{1,0:T(8,128)S(1)} %get-tuple-element.23), channel_id=1, source_target_pairs={{0,1},{1,0},{2,3},{3,2},{4,5},{5,4},{6,7},{7,6},{8,9},{9,8},{10,11... | collective-permute-start | bytes 3080 | tf_op jit(solution)/shard_map/ppermute | solution.py:308
  34.4 5.4 %collective-permute-start.11 = (f32[16,16]{1,0:T(8,128)S(1)}, f32[16,16]{1,0:T(8,128)S(1)}, u32[]{:S(2)}, u32[]{:S(2)}) collective-permute-start(f32[16,16]{1,0:T(8,128)S(1)} %add.12), channel_id=1, source_target_pairs={{0,6},{1,7},{2,4},{3,5},{4,2},{5,3},{6,0},{7,1},{8,14},{9,15},{10,... | collective-permute-start | bytes 3080 | tf_op jit(solution)/shard_map/ppermute | solution.py:308
  37.2 4.6 %collective-permute-start.10 = (f32[16,16]{1,0:T(8,128)S(1)}, f32[16,16]{1,0:T(8,128)S(1)}, u32[]{:S(2)}, u32[]{:S(2)}) collective-permute-start(f32[16,16]{1,0:T(8,128)S(1)} %add.12), channel_id=1, source_target_pairs={{0,4},{1,5},{2,6},{3,7},{4,0},{5,1},{6,2},{7,3},{8,12},{9,13},{10,... | collective-permute-start | bytes 3080 | tf_op jit(solution)/shard_map/ppermute | solution.py:308
  38.0 3.7 %collective-permute-start.9 = (f32[16,16]{1,0:T(8,128)S(1)}, f32[16,16]{1,0:T(8,128)S(1)}, u32[]{:S(2)}, u32[]{:S(2)}) collective-permute-start(f32[16,16]{1,0:T(8,128)S(1)} %add.12), channel_id=1, source_target_pairs={{0,2},{1,3},{2,0},{3,1},{4,6},{5,7},{6,4},{7,5},{8,10},{9,11},{10,... | collective-permute-start | bytes 3080 | tf_op jit(solution)/shard_map/ppermute | solution.py:308
